TPU v7x, 32 devices: a whole 2x2x4 slice. The times are simulated.
32 devices in a mesh: group: 8 (over z, x), shard: 4 (over y, core).
Axes of the slice: x: 2, y: 2, z: 4, core: 2. Of those that a mesh axis runs over, the one named last changes fastest.
Arguments:
- tokens: bfloat16 [64, 1024], P(('group', 'shard')), may hold values from -6 to 6
- norm_gain: float32 [1024], replicated, may hold values from 0.5 to 1.5
- qkv_weight: bfloat16 [1024, 3072], P(None, 'shard'), may hold values from -0.1875 to 0.1875
- conv_weight: float32 [4, 3072], P(None, 'shard'), may hold values from -3 to 3
- conv_state: bfloat16 [64, 3, 3072], P('group', None, 'shard'), may hold values from -6 to 6
- mesa_gates: bfloat16 [1024, 16], replicated, may hold values from -0.1875 to 0.1875
- mesa_bias: float32 [16], replicated, may hold values from -3 to 3
- ridge_term: float32 [8], replicated, may hold values from 0.5 to 2
- key_cache: bfloat16 [128, 128, 1024], P(('group', 'shard')), may hold values from -1.25 to 1.25
- value_cache: bfloat16 [128, 128, 1024], P(('group', 'shard')), may hold values from -6 to 6
- log_weight: bfloat16 [128, 8, 128], P(('group', 'shard'))
- page_owner: int32 [128], P(('group', 'shard')), may hold values from 0 to 15, as said below
- page_fill: int32 [128], P(('group', 'shard')), may hold values from 1 to 128, as said below
- out_weight: bfloat16 [1024, 1024], P('shard'), may hold values from -0.1875 to 0.1875
- mlp_gain: float32 [1024], replicated, may hold values from 0.5 to 1.5
- gate_weight: bfloat16 [1024, 2816], P(None, 'shard'), may hold values from -0.1875 to 0.1875
- up_weight: bfloat16 [1024, 2816], P(None, 'shard'), may hold values from -0.1875 to 0.1875
- down_weight: bfloat16 [2816, 1024], P('shard'), may hold values from -0.109375 to 0.109375
Outputs:
- retrieved: bfloat16 [64, 1024], P(('group', 'shard'))
- layer_out: bfloat16 [64, 1024], P(('group', 'shard'))
Inputs may be any that keep to these rules, and one draw needn't show every extreme that they name: `page_owner`: slots of a pair of groups (groups 2p and 2p + 1) belong to that pair's requests: 0 to 7 are group 2p's requests in row order, 8 to 15 group 2p + 1's. Every slot is owned, every request owns one or more slots, and a request's slots may lie on any device of either group of its pair. `page_fill`: tokens stored from the start of the slot; only a request's last page may be partly filled.
All inputs are finite; a program needn't handle non-finite values.
Results may differ from a plain program's by a relative error of at most 0.0085.
Values may be sent and summed in bfloat16 or wider, within the bound.
No kernel may reach another device: no remote copies, remote signals or barrier semaphores. Data moves between devices by JAX's collectives and lax.ppermute only.
A program may use at most 64 MiB of HBM per device.

v0:
```python
import functools

import jax
import jax.numpy as jnp
from jax import lax
from jax.experimental import pallas as pl
from jax.experimental.pallas import tpu as pltpu
from jax.sharding import Mesh
from jax.sharding import PartitionSpec as P

ITERS = 4


precise = lax.Precision.HIGHEST

VMEM = pl.BlockSpec(memory_space=pltpu.VMEM)
SMEM = pl.BlockSpec(memory_space=pltpu.SMEM)


def partner(value, axis, apart):
    mask = 2**apart
    pairs = [(source, source ^ mask) for source in range(lax.axis_size(axis))]
    return lax.ppermute(value, axis, pairs)


def scaled_norm(row_vals, gain_vec):
    wide_rows = row_vals.astype(jnp.float32)
    factor = lax.rsqrt(jnp.mean(wide_rows * wide_rows, axis=-1, keepdims=True) + 1e-05)
    return (wide_rows * factor * gain_vec).astype(jnp.bfloat16)


def unit_rows(vectors):
    return vectors * lax.rsqrt(jnp.sum(vectors * vectors, axis=-1, keepdims=True) + 1e-06)


def slot_weights(owner_hot, decay_rows, log_weight, page_fill):
    page_len = log_weight.shape[2]
    slot_decay = jnp.dot(owner_hot, decay_rows, precision=precise)
    live_mask = (jnp.arange(page_len)[None, :] < page_fill[:, None]).astype(jnp.float32)
    return slot_decay[:, :, None] * jnp.exp(log_weight.astype(jnp.float32)) * live_mask[:, None, :]


def slot_terms(key_rows, source_rows, owner_hot, slot_weight, directions):
    slot_count, page_len, width_all = key_rows.shape
    head_count = slot_weight.shape[1]
    head_size = width_all // head_count
    member_count = owner_hot.shape[1]
    slot_dir = jnp.dot(owner_hot, directions.reshape(member_count, width_all), precision=precise)
    slot_dir = slot_dir.reshape(slot_count, head_count, head_size)
    key_wide = key_rows.astype(jnp.float32).reshape(slot_count, page_len, head_count, head_size)
    scores = jnp.einsum("sthd,shd->sht", key_wide, slot_dir, precision=precise)
    source_wide = source_rows.astype(jnp.float32).reshape(
        slot_count, page_len, head_count, head_size
    )
    contribution = jnp.einsum("sht,sthd->shd", slot_weight * scores, source_wide, precision=precise)
    summed = jnp.dot(owner_hot.T, contribution.reshape(slot_count, width_all), precision=precise)
    return summed.reshape(member_count, head_count, head_size)


def new_term(vectors, source_rows, strength_rows, key_new):
    return (
        strength_rows[:, :, None] * source_rows * jnp.sum(key_new * vectors, axis=-1, keepdims=True)
    )


def conjugate(query_rows, key_new, value_new, strength_rows, ridge_term, reduce_fn):
    solution = jnp.zeros_like(query_rows)
    residual = query_rows
    direction = query_rows
    res_norm = jnp.sum(residual * residual, axis=-1)
    for iteration in range(ITERS):
        image_vec = (
            reduce_fn(direction, False)
            + new_term(direction, key_new, strength_rows, key_new)
            + ridge_term[None, :, None] * direction
        )
        step_size = res_norm / jnp.sum(direction * image_vec, axis=-1)
        solution = solution + step_size[:, :, None] * direction
        residual = residual - step_size[:, :, None] * image_vec
        next_norm = jnp.sum(residual * residual, axis=-1)
        direction = residual + (next_norm / res_norm)[:, :, None] * direction
        res_norm = next_norm
    return reduce_fn(solution, True) + new_term(solution, value_new, strength_rows, key_new)


def pair_order(mine, theirs, parity):
    first = jnp.where(parity == 0, mine, theirs)
    second = jnp.where(parity == 0, theirs, mine)
    return jnp.concatenate([first, second], axis=0)


def spread_body(
    tokens,
    norm_gain,
    qkv_weight,
    conv_weight,
    conv_state,
    mesa_gates,
    mesa_bias,
    ridge_term,
    key_cache,
    value_cache,
    log_weight,
    page_owner,
    page_fill,
    out_weight,
    mlp_gain,
    gate_weight,
    up_weight,
    down_weight,
):
    req_rows = tokens.shape[0]
    group_rows = req_rows * lax.axis_size("shard")
    head_count = ridge_term.shape[0]
    width_all = key_cache.shape[2]
    head_size = width_all // head_count
    parity = lax.axis_index("group") % 2
    normed = scaled_norm(tokens, norm_gain)
    fresh_proj = jnp.dot(
        lax.all_gather(normed, "shard", axis=0, tiled=True),
        qkv_weight,
        preferred_element_type=jnp.float32,
    )
    past_rows = conv_state.astype(jnp.float32)
    pre_conv = (
        conv_weight[3] * fresh_proj
        + conv_weight[0] * past_rows[:, 0]
        + conv_weight[1] * past_rows[:, 1]
        + conv_weight[2] * past_rows[:, 2]
    )
    mixed_cols = jax.nn.silu(pre_conv).astype(jnp.bfloat16)
    home_rows = lax.all_to_all(mixed_cols, "shard", split_axis=0, concat_axis=1, tiled=True)
    split_rows = home_rows.astype(jnp.float32).reshape(req_rows, 3, head_count, head_size)
    query_home = unit_rows(split_rows[:, 0])
    key_home = unit_rows(split_rows[:, 1])
    value_home = split_rows[:, 2]
    gate_vals = jax.nn.sigmoid(
        jnp.dot(normed, mesa_gates, preferred_element_type=jnp.float32) + mesa_bias
    )
    decay_home = gate_vals[:, :head_count]
    strength_home = gate_vals[:, head_count:]
    owner_hot = (page_owner[:, None] == jnp.arange(2 * group_rows)[None, :]).astype(jnp.float32)
    stored = {}

    def cache_pass(directions, decay_grp, with_values):
        far_dirs, far_decay = partner((directions, decay_grp), "group", 0)
        pair_dirs = pair_order(directions, far_dirs, parity)
        pair_decay = pair_order(decay_grp, far_decay, parity)
        if "weight" not in stored:
            stored["weight"] = slot_weights(owner_hot, pair_decay, log_weight, page_fill)
        source_rows = value_cache if with_values else key_cache
        summed = slot_terms(key_cache, source_rows, owner_hot, stored["weight"], pair_dirs)
        mine = jnp.where(parity == 0, summed[:group_rows], summed[group_rows:])
        theirs = jnp.where(parity == 0, summed[group_rows:], summed[:group_rows])
        returned = partner(theirs, "group", 0)
        return mine + returned

    def reduce_home(vectors, with_values):
        directions, decay_grp = (
            lax.all_gather(vectors, "shard", axis=0, tiled=True),
            lax.all_gather(decay_home, "shard", axis=0, tiled=True),
        )
        return lax.psum_scatter(
            cache_pass(directions, decay_grp, with_values), "shard", scatter_dimension=0, tiled=True
        )

    found = conjugate(query_home, key_home, value_home, strength_home, ridge_term, reduce_home)
    retrieved = found.reshape(req_rows, width_all).astype(jnp.bfloat16)
    columns = lax.all_to_all(retrieved, "shard", split_axis=1, concat_axis=0, tiled=True)
    attended = lax.psum_scatter(
        jnp.dot(columns, out_weight, preferred_element_type=jnp.float32),
        "shard",
        scatter_dimension=0,
        tiled=True,
    )
    mid_rows = (tokens.astype(jnp.float32) + attended).astype(jnp.bfloat16)
    mlp_in = scaled_norm(mid_rows, mlp_gain)
    piece_rows = lax.all_gather(mlp_in, "shard", axis=0, tiled=True)
    gate_part = jnp.dot(piece_rows, gate_weight, preferred_element_type=jnp.float32)
    up_part = jnp.dot(piece_rows, up_weight, preferred_element_type=jnp.float32)
    hidden_rows = (jax.nn.silu(gate_part) * up_part).astype(jnp.bfloat16)
    down_part = lax.psum_scatter(
        jnp.dot(hidden_rows, down_weight, preferred_element_type=jnp.float32),
        "shard",
        scatter_dimension=0,
        tiled=True,
    )
    layer_out = (mid_rows.astype(jnp.float32) + down_part).astype(jnp.bfloat16)
    return (retrieved, layer_out)


TILE = 8
MASKED = -1e38
PAIR = ("shard", "member")
PARAMS = pltpu.CompilerParams(vmem_limit_bytes=16 * 1024 * 1024)
PAST, TAP, GAIN, BIAS, RIDGE = slice(0, 8), slice(8, 9), slice(9, 10), slice(10, 11), slice(11, 12)
GATES = slice(16, 32)

SEND = ((0, 0), (2, 2), (5, 5), (7, 7), (1, 4), (4, 1), (3, 6), (6, 3))
FROM = tuple((b, a) if a & 2 else (a, b) for a, b in SEND)
EARLY = 4


def split_pair(value):
    high = value.astype(jnp.bfloat16)
    low = (value - high.astype(jnp.float32)).astype(jnp.bfloat16)
    return high, low


def hot(rows, columns, target_fn):
    row = lax.broadcasted_iota(jnp.int32, (rows, columns), 0)
    column = lax.broadcasted_iota(jnp.int32, (rows, columns), 1)
    return jnp.where(column == target_fn(row), 1.0, 0.0).astype(jnp.bfloat16)


def here():
    return lax.axis_index("shard") * 2 + lax.axis_index("member")


def at_step(table, step, me):
    return me ^ jnp.where((me & 2) == 0, table[step][0], table[step][1])


def silu(value):
    return value / (1.0 + jnp.exp(-value))


def cut_kernel(key_hbm, value_hbm, *refs):
    *piece_refs, stage_ref, sems = refs
    slots = key_hbm.shape[0]
    head_size = piece_refs[0].shape[2]
    me = here()
    loads = [
        pltpu.make_async_copy(source.at[slot], stage_ref.at[part, slot], sems.at[part * slots + slot])
        for part, source in enumerate((key_hbm, value_hbm))
        for slot in range(slots)
    ]
    for load in loads:
        load.start()
    starts = [
        pl.multiple_of(at_step(SEND, step, me) * head_size, head_size)
        for step in range(len(piece_refs))
    ]
    for part in range(2):
        for slot in range(slots):
            place = part * slots + slot
            loads[place].wait()
            for start, piece_ref in zip(starts, piece_refs):
                piece_ref[place] = stage_ref[part, slot, :, pl.ds(start, head_size)]


def pack_kernel(
    tokens_hbm,
    logs_hbm,
    owner_hbm,
    fill_hbm,
    past_hbm,
    tap_hbm,
    gain_hbm,
    gates_hbm,
    bias_hbm,
    ridge_hbm,
    send_ref,
    misc_ref,
    tokens_ref,
    logs_ref,
    owner_ref,
    fill_ref,
    state_ref,
    gates_ref,
    tap_ref,
    gain_ref,
    bias_ref,
    ridge_ref,
    sems,
):
    req_rows, width = tokens_ref.shape
    slots, head_count, page = logs_ref.shape
    copies = [
        pltpu.make_async_copy(source, target, sems.at[place])
        for place, (source, target) in enumerate(
            [
                (owner_hbm, owner_ref),
                (fill_hbm, fill_ref),
                (tokens_hbm, tokens_ref),
                (logs_hbm, logs_ref),
                (past_hbm, state_ref),
                (tap_hbm, tap_ref),
                (gain_hbm, gain_ref),
                (gates_hbm, gates_ref),
                (bias_hbm, bias_ref),
                (ridge_hbm, ridge_ref),
            ]
        )
    ]
    for copy in copies:
        copy.start()
    for copy in copies:
        copy.wait()

    tokens = tokens_ref[...].astype(jnp.float32)
    rows = [
        tokens[row : row + 1, first : first + page]
        for row in range(req_rows)
        for first in range(0, width, page)
    ]
    tile = jnp.concatenate(rows, axis=0).astype(jnp.bfloat16)
    packed = tile.shape[0] + TILE
    spot = lax.broadcasted_iota(jnp.int32, (head_count, page), 1)
    logs = []
    lane = lax.broadcasted_iota(jnp.int32, (1, page), 1)
    owners = jnp.zeros((1, page), jnp.float32)
    for slot in range(slots):
        rows = logs_ref[slot].astype(jnp.float32)
        logs.append(jnp.where(spot < fill_ref[slot], rows, MASKED))
        owners = jnp.where(lane == slot, owner_ref[slot].astype(jnp.float32), owners)
    rest = jnp.zeros((TILE - slots - 1, page), jnp.float32)
    for head in range(head_count):
        rows = [log[head : head + 1, :] for log in logs]
        side = jnp.concatenate([*rows, owners, rest], axis=0).astype(jnp.bfloat16)
        send_ref[head * packed : head * packed + tile.shape[0], :] = tile
        send_ref[head * packed + tile.shape[0] : (head + 1) * packed, :] = side

    past = tap_ref[0:1, :] * state_ref[0].astype(jnp.float32)
    past = past + tap_ref[1:2, :] * state_ref[1].astype(jnp.float32)
    past = past + tap_ref[2:3, :] * state_ref[2].astype(jnp.float32)
    columns = past.shape[1]
    misc_ref[PAST, :columns] = past
    misc_ref[TAP, :columns] = tap_ref[3:4, :]
    misc_ref[GAIN, :] = gain_ref[...]
    misc_ref[BIAS, : 2 * head_count] = bias_ref[...]
    ridges = jnp.zeros((1, page), jnp.float32)
    for head in range(head_count):
        ridges = jnp.where(lane == head, ridge_ref[head], ridges)
    misc_ref[RIDGE, :page] = ridges
    misc_ref[GATES, :] = gates_ref[...].astype(jnp.float32)


def project_kernel(
    shards,
    req_rows,
    slots,
    head_count,
    pack_ref,
    misc_ref,
    qkv_hbm,
    send_ref,
    tokens_ref,
    weight_ref,
    owner_ref,
    strength_ref,
    mixed_ref,
    qkv_ref,
    sems,
):
    chunk = qkv_ref.shape[0] // sems.shape[0]
    loads = [
        pltpu.make_async_copy(
            qkv_hbm.at[pl.ds(part * chunk, chunk)],
            qkv_ref.at[pl.ds(part * chunk, chunk)],
            sems.at[part],
        )
        for part in range(sems.shape[0])
    ]
    for load in loads:
        load.start()
    shard = lax.axis_index("shard")
    member = lax.axis_index("member")
    head = here()
    group_rows = shards * req_rows
    pair_rows = 2 * group_rows
    width = misc_ref.shape[1]
    columns = qkv_ref.shape[1]
    page = weight_ref.shape[1]
    head_size = send_ref.shape[1]
    blocks = columns // head_size
    parts = width // page
    packed = pack_ref.shape[0]
    tall = packed // (2 * shards)

    def rows_of(first, count):
        def home_of(row):
            request = row % count + first
            x = request // group_rows
            s = (request % group_rows) // req_rows
            return (s * 2 + x) * tall + request % req_rows * parts + row // count

        picked = jnp.dot(
            hot(count * parts, packed, home_of), pack_ref[...], preferred_element_type=jnp.float32
        )
        return jnp.concatenate(
            [picked[part * count : (part + 1) * count] for part in range(parts)], axis=1
        )

    own_tokens = rows_of(member * group_rows, group_rows)
    tokens_ref[...] = own_tokens
    own = scaled_norm(own_tokens, misc_ref[GAIN, :])
    normed = scaled_norm(rows_of(0, pair_rows), misc_ref[GAIN, :])
    raw = lax.dot_general(
        normed,
        misc_ref[GATES, :].astype(jnp.bfloat16),
        (((1,), (1,)), ((), ())),
        preferred_element_type=jnp.float32,
    )
    gate_vals = 1.0 / (1.0 + jnp.exp(-(raw + misc_ref[BIAS, : 2 * head_count])))
    column = lax.broadcasted_iota(jnp.int32, gate_vals.shape, 1)
    decay = jnp.sum(jnp.where(column == head, gate_vals, 0.0), axis=1, keepdims=True)
    strength = jnp.sum(
        jnp.where(column == head + head_count, gate_vals, 0.0), axis=1, keepdims=True
    )
    strength_ref[:pair_rows, :] = jnp.broadcast_to(strength, (pair_rows, head_size))
    ridges = misc_ref[RIDGE, :page]
    spot = lax.broadcasted_iota(jnp.int32, ridges.shape, 1)
    ridge = jnp.sum(jnp.where(spot == head, ridges, 0.0), axis=1, keepdims=True)
    strength_ref[pair_rows:, :] = jnp.broadcast_to(ridge, (TILE, head_size))

    all_slots = 2 * shards * slots
    side = tall - TILE
    pick_slot = hot(all_slots, packed, lambda row: (row // slots) * tall + side + row % slots)
    logs = jnp.dot(pick_slot, pack_ref[...], preferred_element_type=jnp.float32)
    pick_owner = hot(all_slots, packed, lambda row: (row // slots) * tall + side + slots)
    owners = jnp.dot(pick_owner, pack_ref[...], preferred_element_type=jnp.float32)
    at_slot = hot(all_slots, page, lambda row: row % slots).astype(jnp.float32)
    owner = jnp.sum(at_slot * owners, axis=1, keepdims=True).astype(jnp.int32)
    owner_ref[...] = jnp.broadcast_to(owner, owner_ref.shape)
    request = lax.broadcasted_iota(jnp.int32, (all_slots, pair_rows), 1)
    owner_hot = jnp.where(request == owner, 1.0, 0.0)
    wide_decay = jnp.broadcast_to(decay, (pair_rows, page))
    slot_decay = jnp.dot(
        owner_hot, wide_decay, precision=precise, preferred_element_type=jnp.float32
    )
    weight_ref[...] = slot_decay * jnp.exp(logs)

    for load in loads:
        load.wait()
    fresh = jnp.dot(own, qkv_ref[...], preferred_element_type=jnp.float32)
    before = misc_ref[TAP, :columns] * fresh + misc_ref[PAST, :columns]
    mixed_ref[...] = silu(before)
    for target in range(head_count):
        place = jnp.int32(0)
        for part in range(3):
            local = target + part * head_count - shard * blocks
            place = jnp.where((local >= 0) & (local < blocks), local, place)
        start = pl.multiple_of(place * head_size, head_size)
        send_ref[target * group_rows : (target + 1) * group_rows, :] = mixed_ref[
            :, pl.ds(start, head_size)
        ].astype(jnp.bfloat16)


def add_pieces(first, owner_ref, weight_ref, piece_refs, gram_ref):
    me = here()
    slots = piece_refs[0].shape[0] // 2
    for step, piece_ref in enumerate(piece_refs, first):
        for spot in range(slots):
            slot = at_step(FROM, step, me) * slots + spot
            keys = piece_ref[spot]
            both = jnp.concatenate([keys, piece_ref[slots + spot]], axis=1)
            turned = keys.T.astype(jnp.float32) * weight_ref[pl.ds(slot, 1), :]
            piece = jnp.dot(
                jnp.concatenate(split_pair(turned), axis=1),
                jnp.concatenate([both, both], axis=0),
                preferred_element_type=jnp.float32,
            )
            owner = owner_ref[slot, 0]
            gram_ref[owner] = gram_ref[owner] + piece


def gram_kernel(owner_ref, weight_ref, *refs):
    *piece_refs, gram_ref = refs
    gram_ref[...] = jnp.zeros_like(gram_ref)
    add_pieces(0, owner_ref, weight_ref, piece_refs, gram_ref)


def solve_kernel(
    first, head_count, blocks, owner_ref, weight_ref, mixed_ref, strength_ref, before_ref, *refs
):
    *piece_refs, own_ref, other_ref, gram_ref, rows_ref = refs
    head = here()
    member = lax.axis_index("member")
    pair_rows, head_size, _ = gram_ref.shape
    gram_ref[...] = before_ref[...]
    add_pieces(first, owner_ref, weight_ref, piece_refs, gram_ref)

    def columns_of(block):
        first = pl.multiple_of(block // blocks * pair_rows, pair_rows)
        return mixed_ref[pl.ds(first, pair_rows), :].astype(jnp.float32)

    query = unit_rows(columns_of(head))
    key_new = unit_rows(columns_of(head + head_count))
    value_new = columns_of(head + 2 * head_count)
    strength = strength_ref[:pair_rows, :]
    ridge = strength_ref[pair_rows : pair_rows + 1, :]

    def image_of(vectors, columns):
        turned = vectors.T
        pieces = []
        for row in range(pair_rows):
            spread = jnp.broadcast_to(turned[:, row : row + 1], (head_size, head_size))
            pieces.append(jnp.sum(gram_ref[row, :, columns] * spread, axis=0, keepdims=True))
        return jnp.concatenate(pieces, axis=0)

    found = jnp.zeros_like(query)
    residual = query
    direction = query
    res_norm = jnp.sum(residual * residual, axis=-1, keepdims=True)
    for iteration in range(ITERS):
        along = jnp.sum(key_new * direction, axis=-1, keepdims=True)
        image = image_of(direction, slice(0, head_size))
        image = image + strength * key_new * along + ridge * direction
        step = res_norm / jnp.sum(direction * image, axis=-1, keepdims=True)
        found = found + step * direction
        residual = residual - step * image
        next_norm = jnp.sum(residual * residual, axis=-1, keepdims=True)
        direction = residual + (next_norm / res_norm) * direction
        res_norm = next_norm

    total = image_of(found, slice(head_size, 2 * head_size))
    total = total + strength * value_new * jnp.sum(key_new * found, axis=-1, keepdims=True)
    rows_ref[...] = total
    half = pair_rows // 2
    mine = pl.multiple_of(member * half, half)
    theirs = pl.multiple_of((1 - member) * half, half)
    own_ref[...] = rows_ref[pl.ds(mine, half), :].astype(jnp.bfloat16)
    other_ref[...] = rows_ref[pl.ds(theirs, half), :].astype(jnp.bfloat16)


def out_kernel(own_ref, come_ref, out_ref, send_ref):
    first = lax.axis_index("member") == 0
    width = out_ref.shape[1]
    own = own_ref[...].astype(jnp.float32)
    come = come_ref[...].astype(jnp.float32)
    heads = jnp.concatenate([jnp.where(first, own, come), jnp.where(first, come, own)], axis=1)
    heads = heads.astype(jnp.bfloat16)
    part = jnp.dot(heads, out_ref[...], preferred_element_type=jnp.float32)
    send_ref[:, :width] = part.astype(jnp.bfloat16)
    send_ref[:, width:] = heads


def home_rows(value, req_rows):
    first = lax.axis_index("shard") * req_rows
    row = lax.broadcasted_iota(jnp.int32, value.shape, 0)
    picked = [
        jnp.sum(jnp.where(row == first + i, value, 0.0), axis=0, keepdims=True)
        for i in range(req_rows)
    ]
    return jnp.concatenate(picked, axis=0)


def mlp_kernel(
    shards,
    tokens_ref,
    gain_ref,
    gate_ref,
    up_ref,
    down_ref,
    *refs,
):
    part_refs, refs = refs[:shards], refs[shards:]
    mid_ref, retrieved_ref, *send_refs, down_scr, heads_ref = refs
    shard = lax.axis_index("shard")
    group_rows, width = tokens_ref.shape
    req_rows = mid_ref.shape[0]
    span = part_refs[0].shape[1] - width
    attended = part_refs[0][:, :width].astype(jnp.float32)
    for part_ref in part_refs[1:]:
        attended += part_ref[:, :width].astype(jnp.float32)
    mid_rows = (tokens_ref[...] + attended).astype(jnp.bfloat16)
    mlp_in = scaled_norm(mid_rows, gain_ref[...])
    contract = (((1,), (1,)), ((), ()))
    gate_part = lax.dot_general(
        mlp_in, gate_ref[...], contract, preferred_element_type=jnp.float32
    )
    up_part = lax.dot_general(mlp_in, up_ref[...], contract, preferred_element_type=jnp.float32)
    hidden = (silu(gate_part) * up_part).astype(jnp.bfloat16)
    down = jnp.dot(hidden, down_ref[...], preferred_element_type=jnp.float32)
    down_scr[...] = down.reshape(down_scr.shape)
    rows = send_refs[0].shape[0]
    for apart, send_ref in enumerate(send_refs):
        send_ref[...] = down_scr[pl.ds(pl.multiple_of((shard ^ apart) * rows, rows), rows), :]
    mid_ref[...] = home_rows(mid_rows.astype(jnp.float32), mid_ref.shape[0])
    for apart, part_ref in enumerate(part_refs):
        first = pl.multiple_of((shard ^ apart) * span, span)
        heads_ref[:, pl.ds(first, span)] = home_rows(
            part_ref[:, width:].astype(jnp.float32), req_rows
        )
    retrieved_ref[...] = heads_ref[...].astype(jnp.bfloat16)


def finish_kernel(mid_ref, *refs):
    *down_refs, layer_ref = refs
    total = down_refs[0][...]
    for down_ref in down_refs[1:]:
        total = total + down_ref[...]
    layer_ref[...] = (mid_ref[...] + total.reshape(mid_ref.shape)).astype(jnp.bfloat16)


def head_body(
    tokens,
    norm_gain,
    qkv_weight,
    conv_weight,
    conv_state,
    mesa_gates,
    mesa_bias,
    ridge_term,
    key_cache,
    value_cache,
    log_weight,
    page_owner,
    page_fill,
    out_weight,
    mlp_gain,
    gate_weight,
    up_weight,
    down_weight,
):
    shards = lax.axis_size("shard")
    devices = 2 * shards
    req_rows, width = tokens.shape
    slots, page, _ = key_cache.shape
    head_count = ridge_term.shape[0]
    head_size = width // head_count
    group_rows = shards * req_rows
    pair_rows = 2 * group_rows
    all_slots = devices * slots
    columns = qkv_weight.shape[1]
    shape = jax.ShapeDtypeStruct
    bf16, f32 = jnp.bfloat16, jnp.float32

    def exchange(value, axes):
        return lax.all_to_all(value, axes, split_axis=0, concat_axis=0, tiled=True)

    def spot(number):
        return number % 2 * shards + number // 2

    hbm = pl.BlockSpec(memory_space=pltpu.HBM)
    past_rows = jnp.transpose(conv_state, (1, 0, 2))
    gates = mesa_gates.T

    def pinned(*values):
        return [pltpu.with_memory_space_constraint(value, pltpu.HBM) for value in values]

    pieces = pl.pallas_call(
        cut_kernel,
        out_shape=(shape((2 * slots, page, head_size), bf16),) * devices,
        in_specs=[hbm] * 2,
        out_specs=(VMEM,) * devices,
        scratch_shapes=[
            pltpu.VMEM((2, *key_cache.shape), bf16),
            pltpu.SemaphoreType.DMA((2 * slots,)),
        ],
        compiler_params=PARAMS,
        name="cut",
    )(*pinned(key_cache, value_cache))

    def move(step):
        pairs = [
            (spot(source), spot(source ^ SEND[step][source >> 1 & 1])) for source in range(devices)
        ]
        return lax.ppermute(pieces[step], ("member", "shard"), pairs)

    moved = [pieces[0]] + [move(step) for step in range(1, 1 + EARLY)]
    tokens, pieces = lax.optimization_barrier((tokens, pieces))
    pack, misc = pl.pallas_call(
        pack_kernel,
        out_shape=(
            shape((devices * (req_rows * width // page + TILE), page), bf16),
            shape((GATES.stop, width), f32),
        ),
        in_specs=[hbm] * 10,
        out_specs=(VMEM,) * 2,
        scratch_shapes=[
            pltpu.VMEM(tokens.shape, bf16),
            pltpu.VMEM(log_weight.shape, bf16),
            pltpu.SMEM(page_owner.shape, jnp.int32),
            pltpu.SMEM(page_fill.shape, jnp.int32),
            pltpu.VMEM(past_rows.shape, bf16),
            pltpu.VMEM(gates.shape, bf16),
            pltpu.VMEM(conv_weight.shape, f32),
            pltpu.VMEM((1, width), f32),
            pltpu.VMEM((1, 2 * head_count), f32),
            pltpu.SMEM(ridge_term.shape, f32),
            pltpu.SemaphoreType.DMA((10,)),
        ],
        compiler_params=PARAMS,
        name="pack",
    )(
        *pinned(
            tokens,
            log_weight,
            page_owner,
            page_fill,
            past_rows,
            conv_weight,
            norm_gain[None, :],
            gates,
            mesa_bias[None, :],
            ridge_term,
        )
    )
    packs = exchange(pack, PAIR)

    pieces, packs = lax.optimization_barrier((pieces, packs))
    moved += [move(step) for step in range(1 + EARLY, devices)]

    mixed, own_tokens, weight, owner, strength = pl.pallas_call(
        functools.partial(project_kernel, shards, req_rows, slots, head_count),
        out_shape=(
            shape((devices * group_rows, head_size), bf16),
            shape((group_rows, width), f32),
            shape((all_slots, page), f32),
            shape((all_slots, page), jnp.int32),
            shape((pair_rows + TILE, head_size), f32),
        ),
        in_specs=[VMEM] * 2 + [hbm],
        out_specs=(VMEM,) * 5,
        scratch_shapes=[
            pltpu.VMEM((group_rows, columns), f32),
            pltpu.VMEM(qkv_weight.shape, bf16),
            pltpu.SemaphoreType.DMA((4,)),
        ],
        compiler_params=PARAMS,
        name="project",
    )(packs, misc, *pinned(qkv_weight))

    held = 1 + EARLY
    gram = pl.pallas_call(
        gram_kernel,
        out_shape=shape((pair_rows, head_size, 2 * head_size), f32),
        in_specs=[SMEM] + [VMEM] * (1 + held),
        out_specs=VMEM,
        compiler_params=PARAMS,
        name="gram",
    )(owner, weight, *moved[:held])
    mixed, gram = lax.optimization_barrier((mixed, gram))
    all_mixed = exchange(mixed, PAIR)
    all_mixed, owner, weight, gram = lax.optimization_barrier((all_mixed, owner, weight, gram))

    own_head, other_head = pl.pallas_call(
        functools.partial(solve_kernel, held, head_count, columns // head_size),
        out_shape=(shape((group_rows, head_size), bf16),) * 2,
        in_specs=[SMEM] + [VMEM] * (4 + devices - held),
        out_specs=(VMEM,) * 2,
        scratch_shapes=[
            pltpu.VMEM((pair_rows, head_size, 2 * head_size), f32),
            pltpu.VMEM((pair_rows, head_size), f32),
        ],
        compiler_params=PARAMS,
        name="solve",
    )(owner, weight, all_mixed, strength, gram, *moved[held:])
    part = pl.pallas_call(
        out_kernel,
        out_shape=shape((group_rows, width + 2 * head_size), bf16),
        in_specs=[VMEM] * 3,
        out_specs=VMEM,
        compiler_params=PARAMS,
        name="out",
    )(own_head, lax.ppermute(other_head, "member", [(0, 1), (1, 0)]), out_weight)

    def over_shards(sent):
        arrived = [sent[0]]
        for apart in range(1, shards):
            pairs = [(source, source ^ apart) for source in range(shards)]
            arrived.append(lax.ppermute(sent[apart], "shard", pairs))
        return arrived

    parts = over_shards([part] * shards)

    mid_home, retrieved, *down = pl.pallas_call(
        functools.partial(mlp_kernel, shards),
        out_shape=(
            shape((req_rows, width), f32),
            shape((req_rows, width), bf16),
        )
        + (shape((req_rows * head_count, head_size), f32),) * shards,
        in_specs=[VMEM] * (5 + shards),
        out_specs=(VMEM,) * (2 + shards),
        scratch_shapes=[
            pltpu.VMEM((group_rows * head_count, head_size), f32),
            pltpu.VMEM((req_rows, width), f32),
        ],
        compiler_params=PARAMS,
        name="mlp",
    )(
        own_tokens,
        mlp_gain[None, :],
        gate_weight.T,
        up_weight.T,
        down_weight,
        *parts,
    )
    layer_out = pl.pallas_call(
        finish_kernel,
        out_shape=shape((req_rows, width), bf16),
        in_specs=[VMEM] * (1 + shards),
        out_specs=VMEM,
        compiler_params=PARAMS,
        name="finish",
    )(mid_home, *over_shards(down))
    return (retrieved, layer_out)


def specs(group):
    rows = P((*group, "shard"))
    return (
        (
            rows,
            P(),
            P(None, "shard"),
            P(None, "shard"),
            P(group, None, "shard"),
            P(),
            P(),
            P(),
            rows,
            rows,
            rows,
            rows,
            rows,
            P("shard", None),
            P(),
            P(None, "shard"),
            P(None, "shard"),
            P("shard", None),
        ),
        (rows, rows),
    )


def solution(mesh):
    groups, shards = mesh.devices.shape

    def run(*args):
        head_count = args[7].shape[0]
        if 2 * shards == head_count == len(SEND):
            axes = ("pair", "member", "shard")
            used = Mesh(mesh.devices.reshape(groups // 2, 2, shards), axes)
            body, group = head_body, ("pair", "member")
        else:
            used, body, group = mesh, spread_body, ("group",)
        in_specs, out_specs = specs(group)
        return jax.shard_map(
            body, mesh=used, in_specs=in_specs, out_specs=out_specs, check_vma=False
        )(*args)

    return run
```

profile of v0, /device:TPU:0, one launch (start us, length us, event | category | flops | bytes accessed | tf_op | source)
XLA Modules:
  0.0 54.4 jit_solution(7767839807173888105)
XLA Ops:
  0.6 1.6 %cut.1 = (bf16[8,128,128]{2,1,0:T(8,128)(2,1)S(1)}, bf16[8,128,128]{2,1,0:T(8,128)(2,1)S(1)}, bf16[8,128,128]{2,1,0:T(8,128)(2,1)S(1)}, bf16[8,128,128]{2,1,0:T(...) custom-call(bf16[4,128,1024]{2,1,0:T(8,128)(2,1)} %key_hbm.1, ...), custom_call_target="tpu_custom_call" | custom-call | tf_op jit(solution)/shard_map/cut/pallas_call | solution.py:643
  2.8 3.5 %collective-permute-start.1 = (bf16[8,128,128]{2,1,0:T(8,128)(2,1)S(1)}, bf16[8,128,128]{2,1,0:T(8,128)(2,1)S(1)}, u32[]{:S(2)}, u32[]{:S(2)}) collective-permute-start(bf16[8,128,128]{2,1,0:T(8,128)(2,1)S(1)} %get-tuple-element.41), channel_id=1, source_target_pairs={{0,6},{4,2},{1,7},{5,3},{2,4},{6,0},{3,5},{7,1},{8,14},{12,10},{9,... | collective-permute-start | bytes 786440 | tf_op jit(solution)/shard_map/ppermute | solution.py:660
  6.3 1.6 %pack.1 = (bf16[192,128]{1,0:T(8,128)(2,1)}, f32[32,1024]{1,0:T(8,128)S(1)}) custom-call(bf16[2,1024]{1,0:T(2,128)(2,1)} %tokens_hbm, bf16[4,8,128]{2,1,0:T(8,128)(2,1)} %logs_hbm.1, s32[4]{0:T(128)} %owner_hbm.1, s32[4]{0:T(128)} %fill_hbm.1, bf16[3,8,768]{2,1,0:T(8,128)(2,1)} %bitcast.17, f32[4,768]{1,0:T(4,128)} %tap_hbm.1, f32[1,1024]{1,0:T(1,128)} %bitcast.19, ...), custom_call_target="tpu_custom_call" | custom-call | tf_op jit(solution)/shard_map/pack/pallas_call | solution.py:664
  7.9 3.4 %all-to-all-start = ((bf16[8,24,128]{2,1,0:T(8,128)(2,1)}), bf16[8,24,128]{2,1,0:T(8,128)(2,1)S(1)}, u32[]{:S(2)}, u32[]{:S(2)}) async-start(bf16[8,24,128]{2,1,0:T(8,128)(2,1)} %bitcast.4), calls=%async_computation | async-start | bytes 98304 | tf_op jit(solution)/shard_map/all_to_all | solution.py:631
  11.3 2.6 %collective-permute-start.2 = (bf16[8,128,128]{2,1,0:T(8,128)(2,1)S(1)}, bf16[8,128,128]{2,1,0:T(8,128)(2,1)S(1)}, u32[]{:S(2)}, u32[]{:S(2)}) collective-permute-start(bf16[8,128,128]{2,1,0:T(8,128)(2,1)S(1)} %get-tuple-element.42), channel_id=1, source_target_pairs={{0,7},{4,3},{1,6},{5,2},{2,5},{6,1},{3,4},{7,0},{8,15},{12,11},{9,... | collective-permute-start | bytes 786440 | tf_op jit(solution)/shard_map/ppermute | solution.py:660
  14.4 1.6 %all-to-all-done = bf16[8,24,128]{2,1,0:T(8,128)(2,1)S(1)} async-done(((bf16[8,24,128]{2,1,0:T(8,128)(2,1)}), bf16[8,24,128]{2,1,0:T(8,128)(2,1)S(1)}, u32[]{:S(2)}, u32[]{:S(2)}) %all-to-all-start) | async-done | bytes 49184 | tf_op jit(solution)/shard_map/all_to_all | solution.py:631
  16.5 1.1 %collective-permute-start.5 = (bf16[8,128,128]{2,1,0:T(8,128)(2,1)S(1)}, bf16[8,128,128]{2,1,0:T(8,128)(2,1)S(1)}, u32[]{:S(2)}, u32[]{:S(2)}) collective-permute-start(bf16[8,128,128]{2,1,0:T(8,128)(2,1)S(1)} %get-tuple-element.66), channel_id=1, source_target_pairs={{0,5},{4,1},{1,2},{5,6},{2,7},{6,3},{3,0},{7,4},{8,13},{12,9},{9,1... | collective-permute-start | bytes 786440 | tf_op jit(solution)/shard_map/ppermute | solution.py:660
  17.7 0.6 %collective-permute-start.6 = (bf16[8,128,128]{2,1,0:T(8,128)(2,1)S(1)}, bf16[8,128,128]{2,1,0:T(8,128)(2,1)S(1)}, u32[]{:S(2)}, u32[]{:S(2)}) collective-permute-start(bf16[8,128,128]{2,1,0:T(8,128)(2,1)S(1)} %get-tuple-element.67), channel_id=1, source_target_pairs={{0,3},{4,7},{1,4},{5,0},{2,1},{6,5},{3,6},{7,2},{8,11},{12,15},{9,... | collective-permute-start | bytes 786440 | tf_op jit(solution)/shard_map/ppermute | solution.py:660
  18.3 1.9 %project.1 = (bf16[64,128]{1,0:T(8,128)(2,1)S(1)}, f32[8,1024]{1,0:T(8,128)S(1)}, f32[32,128]{1,0:T(8,128)S(1)}, s32[32,128]{1,0:T(8,128)S(1)}, f32[24,128]{1,0:T(8,128)S(1)}) custom-call(bf16[192,128]{1,0:T(8,128)(2,1)S(1)} %bitcast.13, f32[32,1024]{1,0:T(8,128)S(1)} %get-tuple-element.53.misc_ref, bf16[1024,768]{1,0:T(8,128)(2,1)} %qkv_hbm.1), custom_call_target="tpu_custom_call" | custom-call | tf_op jit(solution)/shard_map/project/pallas_call | solution.py:706
  20.2 0.9 %collective-permute-done.2.refs_3_ = bf16[8,128,128]{2,1,0:T(8,128)(2,1)S(1)} collective-permute-done((bf16[8,128,128]{2,1,0:T(8,128)(2,1)S(1)}, bf16[8,128,128]{2,1,0:T(8,128)(2,1)S(1)}, u32[]{:S(2)}, u32[]{:S(2)}) %collective-permute-start.2) | collective-permute-done | bytes 262176 | tf_op jit(solution)/shard_map/ppermute | solution.py:660
  21.1 6.2 %collective-permute-done.3.refs_4_ = bf16[8,128,128]{2,1,0:T(8,128)(2,1)S(1)} collective-permute-done((bf16[8,128,128]{2,1,0:T(8,128)(2,1)S(1)}, bf16[8,128,128]{2,1,0:T(8,128)(2,1)S(1)}, u32[]{:S(2)}, u32[]{:S(2)}) %collective-permute-start.3) | collective-permute-done | bytes 262176 | tf_op jit(solution)/shard_map/ppermute | solution.py:660
  27.2 1.6 %gram.1.before_ref = f32[16,128,256]{2,1,0:T(8,128)S(1)} custom-call(s32[32,128]{1,0:T(8,128)S(1)} %get-tuple-element.60.owner_ref, f32[32,128]{1,0:T(8,128)S(1)} %get-tuple-element.61.weight_ref, bf16[8,128,128]{2,1,0:T(8,128)(2,1)S(1)} %get-tuple-element.39.refs_0_, bf16[8,128,128]{2,1,0:T(8,128)(2,1)S(1)} %collective-permute-done.refs_1_, ...), custom_call_target="tpu_custom_call" | custom-call | tf_op jit(solution)/shard_map/gram/pallas_call | solution.py:727
  28.8 7.3 %all_to_all.24 = bf16[8,8,128]{2,1,0:T(8,128)(2,1)S(1)} all-to-all(bf16[8,8,128]{2,1,0:T(8,128)(2,1)S(1)} %bitcast.15), channel_id=1, replica_groups=mesh['pair'=4,'member'=2,'shard'=4] {'shard','member'}, dimensions={0} | all-to-all | bytes 32768 | tf_op jit(solution)/shard_map/all_to_all | solution.py:631
  36.1 4.2 %solve.1 = (bf16[8,128]{1,0:T(8,128)(2,1)S(1)}, bf16[8,128]{1,0:T(8,128)(2,1)S(1)}) custom-call(s32[32,128]{1,0:T(8,128)S(1)} %get-tuple-element.60.owner_ref, f32[32,128]{1,0:T(8,128)S(1)} %get-tuple-element.61.weight_ref, bf16[64,128]{1,0:T(8,128)(2,1)S(1)} %bitcast.14, f32[24,128]{1,0:T(8,128)S(1)} %get-tuple-element.63.strength_ref, ...), custom_call_target="tpu_custom_call" | custom-call | tf_op jit(solution)/shard_map/solve/pallas_call | solution.py:739
  40.3 0.7 %collective-permute-start.7 = (bf16[8,128]{1,0:T(8,128)(2,1)S(1)}, bf16[8,128]{1,0:T(8,128)(2,1)S(1)}, u32[]{:S(2)}, u32[]{:S(2)}) collective-permute-start(bf16[8,128]{1,0:T(8,128)(2,1)S(1)} %get-tuple-element.69), channel_id=1, source_target_pairs={{0,4},{4,0},{1,5},{5,1},{2,6},{6,2},{3,7},{7,3},{8,12},{12,8},{9,1... | collective-permute-start | bytes 6152 | tf_op jit(solution)/shard_map/ppermute | solution.py:758
  41.0 3.0 %collective-permute-done.7.come_ref = bf16[8,128]{1,0:T(8,128)(2,1)S(1)} collective-permute-done((bf16[8,128]{1,0:T(8,128)(2,1)S(1)}, bf16[8,128]{1,0:T(8,128)(2,1)S(1)}, u32[]{:S(2)}, u32[]{:S(2)}) %collective-permute-start.7) | collective-permute-done | bytes 2080 | tf_op jit(solution)/shard_map/ppermute | solution.py:758
  44.1 0.6 %collective-permute-start.9 = (bf16[8,1280]{1,0:T(8,128)(2,1)S(1)}, bf16[8,1280]{1,0:T(8,128)(2,1)S(1)}, u32[]{:S(2)}, u32[]{:S(2)}) collective-permute-start(bf16[8,1280]{1,0:T(8,128)(2,1)S(1)} %out.1.refs_0_), channel_id=1, source_target_pairs={{0,2},{1,3},{2,0},{3,1},{4,6},{5,7},{6,4},{7,5},{8,10},{9,11},{10,... | collective-permute-start | bytes 61448 | tf_op jit(solution)/shard_map/ppermute | solution.py:764
  44.8 1.3 %collective-permute-start.8 = (bf16[8,1280]{1,0:T(8,128)(2,1)S(1)}, bf16[8,1280]{1,0:T(8,128)(2,1)S(1)}, u32[]{:S(2)}, u32[]{:S(2)}) collective-permute-start(bf16[8,1280]{1,0:T(8,128)(2,1)S(1)} %out.1.refs_0_), channel_id=1, source_target_pairs={{0,1},{1,0},{2,3},{3,2},{4,5},{5,4},{6,7},{7,6},{8,9},{9,8},{10,11... | collective-permute-start | bytes 61448 | tf_op jit(solution)/shard_map/ppermute | solution.py:764
  46.0 1.3 %collective-permute-done.10.refs_3_ = bf16[8,1280]{1,0:T(8,128)(2,1)S(1)} collective-permute-done((bf16[8,1280]{1,0:T(8,128)(2,1)S(1)}, bf16[8,1280]{1,0:T(8,128)(2,1)S(1)}, u32[]{:S(2)}, u32[]{:S(2)}) %collective-permute-start.10) | collective-permute-done | bytes 20512 | tf_op jit(solution)/shard_map/ppermute | solution.py:764
  47.4 0.6 %collective-permute-done.9.refs_2_ = bf16[8,1280]{1,0:T(8,128)(2,1)S(1)} collective-permute-done((bf16[8,1280]{1,0:T(8,128)(2,1)S(1)}, bf16[8,1280]{1,0:T(8,128)(2,1)S(1)}, u32[]{:S(2)}, u32[]{:S(2)}) %collective-permute-start.9) | collective-permute-done | bytes 20512 | tf_op jit(solution)/shard_map/ppermute | solution.py:764
  48.0 1.7 %mlp.1 = (f32[2,1024]{1,0:T(2,128)S(1)}, bf16[2,1024]{1,0:T(2,128)(2,1)}, f32[16,128]{1,0:T(8,128)S(1)}, f32[16,128]{1,0:T(8,128)S(1)}, f32[16,128]{1,0:T(8,128)S(1)}, /*index=5*/f32[16,128]{1,0:T(8,128)S(1)}) custom-call(f32[8,1024]{1,0:T(8,128)S(1)} %get-tuple-element.54.tokens_ref, f32[1,1024]{1,0:T(1,128)S(1)} %bitcast.16, ...), custom_call_target="tpu_custom_call" | custom-call | tf_op jit(solution)/shard_map/mlp/pallas_call | solution.py:769
  49.7 0.9 %collective-permute-start.12 = (f32[16,128]{1,0:T(8,128)S(1)}, f32[16,128]{1,0:T(8,128)S(1)}, u32[]{:S(2)}, u32[]{:S(2)}) collective-permute-start(f32[16,128]{1,0:T(8,128)S(1)} %get-tuple-element.74), channel_id=1, source_target_pairs={{0,2},{1,3},{2,0},{3,1},{4,6},{5,7},{6,4},{7,5},{8,10},{9,11},{10,... | collective-permute-start | bytes 24584 | tf_op jit(solution)/shard_map/ppermute | solution.py:764
  50.6 0.9 %collective-permute-start.13 = (f32[16,128]{1,0:T(8,128)S(1)}, f32[16,128]{1,0:T(8,128)S(1)}, u32[]{:S(2)}, u32[]{:S(2)}) collective-permute-start(f32[16,128]{1,0:T(8,128)S(1)} %get-tuple-element.75), channel_id=1, source_target_pairs={{0,3},{1,2},{2,1},{3,0},{4,7},{5,6},{6,5},{7,4},{8,11},{9,10},{10,... | collective-permute-start | bytes 24584 | tf_op jit(solution)/shard_map/ppermute | solution.py:764
  51.5 1.8 %collective-permute-done.12.refs_2_ = f32[16,128]{1,0:T(8,128)S(1)} collective-permute-done((f32[16,128]{1,0:T(8,128)S(1)}, f32[16,128]{1,0:T(8,128)S(1)}, u32[]{:S(2)}, u32[]{:S(2)}) %collective-permute-start.12) | collective-permute-done | bytes 8224 | tf_op jit(solution)/shard_map/ppermute | solution.py:764
  (25 shorter events, 2.8 us)
Async XLA Ops:
  2.3 14.2 %collective-permute-start = (bf16[8,128,128]{2,1,0:T(8,128)(2,1)S(1)}, bf16[8,128,128]{2,1,0:T(8,128)(2,1)S(1)}, u32[]{:S(2)}, u32[]{:S(2)}) collective-permute-start(bf16[8,128,128]{2,1,0:T(8,128)(2,1)S(1)} %get-tuple-element.40), channel_id=1, source_target_pairs={{0,1},{4,5},{1,0},{5,4},{2,3},{6,7},{3,2},{7,6},{8,9},{12,13},{9,8... | collective-permute-start | bytes 786440 | tf_op jit(solution)/shard_map/ppermute | solution.py:660
  2.8 14.9 %collective-permute-start.1 = (bf16[8,128,128]{2,1,0:T(8,128)(2,1)S(1)}, bf16[8,128,128]{2,1,0:T(8,128)(2,1)S(1)}, u32[]{:S(2)}, u32[]{:S(2)}) collective-permute-start(bf16[8,128,128]{2,1,0:T(8,128)(2,1)S(1)} %get-tuple-element.41), channel_id=1, source_target_pairs={{0,6},{4,2},{1,7},{5,3},{2,4},{6,0},{3,5},{7,1},{8,14},{12,10},{9,... | collective-permute-start | bytes 786440 | tf_op jit(solution)/shard_map/ppermute | solution.py:660
  7.9 8.1 %all-to-all-start = ((bf16[8,24,128]{2,1,0:T(8,128)(2,1)}), bf16[8,24,128]{2,1,0:T(8,128)(2,1)S(1)}, u32[]{:S(2)}, u32[]{:S(2)}) async-start(bf16[8,24,128]{2,1,0:T(8,128)(2,1)} %bitcast.4), calls=%async_computation | async-start | bytes 98304 | tf_op jit(solution)/shard_map/all_to_all | solution.py:631
  11.3 9.8 %collective-permute-start.2 = (bf16[8,128,128]{2,1,0:T(8,128)(2,1)S(1)}, bf16[8,128,128]{2,1,0:T(8,128)(2,1)S(1)}, u32[]{:S(2)}, u32[]{:S(2)}) collective-permute-start(bf16[8,128,128]{2,1,0:T(8,128)(2,1)S(1)} %get-tuple-element.42), channel_id=1, source_target_pairs={{0,7},{4,3},{1,6},{5,2},{2,5},{6,1},{3,4},{7,0},{8,15},{12,11},{9,... | collective-permute-start | bytes 786440 | tf_op jit(solution)/shard_map/ppermute | solution.py:660
  13.9 13.4 %collective-permute-start.3 = (bf16[8,128,128]{2,1,0:T(8,128)(2,1)S(1)}, bf16[8,128,128]{2,1,0:T(8,128)(2,1)S(1)}, u32[]{:S(2)}, u32[]{:S(2)}) collective-permute-start(bf16[8,128,128]{2,1,0:T(8,128)(2,1)S(1)} %get-tuple-element.43), channel_id=1, source_target_pairs={{0,4},{4,0},{1,3},{5,7},{2,6},{6,2},{3,1},{7,5},{8,12},{12,8},{9,1... | collective-permute-start | bytes 786440 | tf_op jit(solution)/shard_map/ppermute | solution.py:660
  16.1 20.0 %collective-permute-start.4 = (bf16[8,128,128]{2,1,0:T(8,128)(2,1)S(1)}, bf16[8,128,128]{2,1,0:T(8,128)(2,1)S(1)}, u32[]{:S(2)}, u32[]{:S(2)}) collective-permute-start(bf16[8,128,128]{2,1,0:T(8,128)(2,1)S(1)} %get-tuple-element.65), channel_id=1, source_target_pairs={{0,2},{4,6},{1,5},{5,1},{2,0},{6,4},{3,7},{7,3},{8,10},{12,14},{9,... | collective-permute-start | bytes 786440 | tf_op jit(solution)/shard_map/ppermute | solution.py:660
  16.5 19.5 %collective-permute-start.5 = (bf16[8,128,128]{2,1,0:T(8,128)(2,1)S(1)}, bf16[8,128,128]{2,1,0:T(8,128)(2,1)S(1)}, u32[]{:S(2)}, u32[]{:S(2)}) collective-permute-start(bf16[8,128,128]{2,1,0:T(8,128)(2,1)S(1)} %get-tuple-element.66), channel_id=1, source_target_pairs={{0,5},{4,1},{1,2},{5,6},{2,7},{6,3},{3,0},{7,4},{8,13},{12,9},{9,1... | collective-permute-start | bytes 786440 | tf_op jit(solution)/shard_map/ppermute | solution.py:660
  17.7 18.4 %collective-permute-start.6 = (bf16[8,128,128]{2,1,0:T(8,128)(2,1)S(1)}, bf16[8,128,128]{2,1,0:T(8,128)(2,1)S(1)}, u32[]{:S(2)}, u32[]{:S(2)}) collective-permute-start(bf16[8,128,128]{2,1,0:T(8,128)(2,1)S(1)} %get-tuple-element.67), channel_id=1, source_target_pairs={{0,3},{4,7},{1,4},{5,0},{2,1},{6,5},{3,6},{7,2},{8,11},{12,15},{9,... | collective-permute-start | bytes 786440 | tf_op jit(solution)/shard_map/ppermute | solution.py:660
  27.2 16.7 %copy-start.3 = (bf16[256,1024]{1,0:T(8,128)(2,1)S(1)}, bf16[256,1024]{1,0:T(8,128)(2,1)}, u32[]{:S(2)}) copy-start(bf16[256,1024]{1,0:T(8,128)(2,1)} %out_ref.1) | copy-start | bytes 1572868
  27.2 20.7 %copy-start.2 = (bf16[704,1024]{1,0:T(8,128)(2,1)S(1)}, bf16[704,1024]{1,0:T(8,128)(2,1)}, u32[]{:S(2)}) copy-start(bf16[704,1024]{1,0:T(8,128)(2,1)} %down_ref.1) | copy-start | bytes 4325380
  36.1 11.9 %copy-start = (bf16[1024,704]{0,1:T(8,128)(2,1)S(1)}, bf16[1024,704]{0,1:T(8,128)(2,1)}, u32[]{:S(2)}) copy-start(bf16[1024,704]{0,1:T(8,128)(2,1)} %param.33) | copy-start | bytes 4325380
  36.1 11.9 %copy-start.1 = (bf16[1024,704]{0,1:T(8,128)(2,1)S(1)}, bf16[1024,704]{0,1:T(8,128)(2,1)}, u32[]{:S(2)}) copy-start(bf16[1024,704]{0,1:T(8,128)(2,1)} %param.34) | copy-start | bytes 4325380
  36.1 11.9 %copy-start.4 = (f32[1024]{0:T(1024)S(1)}, f32[1024]{0:T(1024)}, u32[]{:S(2)}) copy-start(f32[1024]{0:T(1024)} %param.32) | copy-start | bytes 12292
  40.3 3.6 %collective-permute-start.7 = (bf16[8,128]{1,0:T(8,128)(2,1)S(1)}, bf16[8,128]{1,0:T(8,128)(2,1)S(1)}, u32[]{:S(2)}, u32[]{:S(2)}) collective-permute-start(bf16[8,128]{1,0:T(8,128)(2,1)S(1)} %get-tuple-element.69), channel_id=1, source_target_pairs={{0,4},{4,0},{1,5},{5,1},{2,6},{6,2},{3,7},{7,3},{8,12},{12,8},{9,1... | collective-permute-start | bytes 6152 | tf_op jit(solution)/shard_map/ppermute | solution.py:758
  44.1 3.2 %collective-permute-start.10 = (bf16[8,1280]{1,0:T(8,128)(2,1)S(1)}, bf16[8,1280]{1,0:T(8,128)(2,1)S(1)}, u32[]{:S(2)}, u32[]{:S(2)}) collective-permute-start(bf16[8,1280]{1,0:T(8,128)(2,1)S(1)} %out.1.refs_0_), channel_id=1, source_target_pairs={{0,3},{1,2},{2,1},{3,0},{4,7},{5,6},{6,5},{7,4},{8,11},{9,10},{10,... | collective-permute-start | bytes 61448 | tf_op jit(solution)/shard_map/ppermute | solution.py:764
  44.1 3.8 %collective-permute-start.9 = (bf16[8,1280]{1,0:T(8,128)(2,1)S(1)}, bf16[8,1280]{1,0:T(8,128)(2,1)S(1)}, u32[]{:S(2)}, u32[]{:S(2)}) collective-permute-start(bf16[8,1280]{1,0:T(8,128)(2,1)S(1)} %out.1.refs_0_), channel_id=1, source_target_pairs={{0,2},{1,3},{2,0},{3,1},{4,6},{5,7},{6,4},{7,5},{8,10},{9,11},{10,... | collective-permute-start | bytes 61448 | tf_op jit(solution)/shard_map/ppermute | solution.py:764
  44.8 3.2 %collective-permute-start.8 = (bf16[8,1280]{1,0:T(8,128)(2,1)S(1)}, bf16[8,1280]{1,0:T(8,128)(2,1)S(1)}, u32[]{:S(2)}, u32[]{:S(2)}) collective-permute-start(bf16[8,1280]{1,0:T(8,128)(2,1)S(1)} %out.1.refs_0_), channel_id=1, source_target_pairs={{0,1},{1,0},{2,3},{3,2},{4,5},{5,4},{6,7},{7,6},{8,9},{9,8},{10,11... | collective-permute-start | bytes 61448 | tf_op jit(solution)/shard_map/ppermute | solution.py:764
  49.7 1.9 %collective-permute-start.11 = (f32[16,128]{1,0:T(8,128)S(1)}, f32[16,128]{1,0:T(8,128)S(1)}, u32[]{:S(2)}, u32[]{:S(2)}) collective-permute-start(f32[16,128]{1,0:T(8,128)S(1)} %get-tuple-element.73), channel_id=1, source_target_pairs={{0,1},{1,0},{2,3},{3,2},{4,5},{5,4},{6,7},{7,6},{8,9},{9,8},{10,11... | collective-permute-start | bytes 24584 | tf_op jit(solution)/shard_map/ppermute | solution.py:764
  49.7 3.7 %collective-permute-start.12 = (f32[16,128]{1,0:T(8,128)S(1)}, f32[16,128]{1,0:T(8,128)S(1)}, u32[]{:S(2)}, u32[]{:S(2)}) collective-permute-start(f32[16,128]{1,0:T(8,128)S(1)} %get-tuple-element.74), channel_id=1, source_target_pairs={{0,2},{1,3},{2,0},{3,1},{4,6},{5,7},{6,4},{7,5},{8,10},{9,11},{10,... | collective-permute-start | bytes 24584 | tf_op jit(solution)/shard_map/ppermute | solution.py:764
  50.6 3.1 %collective-permute-start.13 = (f32[16,128]{1,0:T(8,128)S(1)}, f32[16,128]{1,0:T(8,128)S(1)}, u32[]{:S(2)}, u32[]{:S(2)}) collective-permute-start(f32[16,128]{1,0:T(8,128)S(1)} %get-tuple-element.75), channel_id=1, source_target_pairs={{0,3},{1,2},{2,1},{3,0},{4,7},{5,6},{6,5},{7,4},{8,11},{9,10},{10,... | collective-permute-start | bytes 24584 | tf_op jit(solution)/shard_map/ppermute | solution.py:764
where the time goes:
time: 54.7 us; the launch traced here: 54.4 us
  starting transfers between devices  17.2 us (31%)
  waiting for transfers between devices  15.8 us (29%)
  Pallas kernels  13.3 us (24%)
  blocking collectives  7.25 us (13%)
  between operations  0.73 us (1%)
    ppermute x7, starting transfers between devices, move(): return lax.ppermute(pieces[step], ('member', 'shard'), pairs)  9.42 us
    all_to_all x1, blocking collectives, exchange(): return lax.all_to_all(value, axes, split_axis=0, concat_axis=0, tiled=True)  7.25 us
    ppermute x7, waiting for transfers between devices, move(): return lax.ppermute(pieces[step], ('member', 'shard'), pairs)  7.04 us
    ppermute x6, waiting for transfers between devices, over_shards(): arrived.append(lax.ppermute(sent[apart], 'shard', pairs))  4.19 us
    pallas_call x1, Pallas kernels, head_body(): pl.pallas_call(functools.partial(solve_kernel, held, head_count, columns...  4.19 us
    ppermute x6, starting transfers between devices, over_shards(): arrived.append(lax.ppermute(sent[apart], 'shard', pairs))  3.74 us
    all_to_all x1, starting transfers between devices, exchange(): return lax.all_to_all(value, axes, split_axis=0, concat_axis=0, tiled=True)  3.36 us
    ppermute x1, waiting for transfers between devices, head_body(): lax.ppermute(other_head, 'member', [(0, 1), (1, 0)])  2.98 us
  transfers between devices with their start and end apart: 15, of which 8 were waited for; matrix products, arithmetic and copies ran while one was open for 0% of the time, Pallas kernels for 9%

commit v1 on v0

--- a/solution.py
+++ b/solution.py
@@ -199,6 +199,7 @@
 SEND = ((0, 0), (2, 2), (5, 5), (7, 7), (1, 4), (4, 1), (3, 6), (6, 3))
 FROM = tuple((b, a) if a & 2 else (a, b) for a, b in SEND)
 EARLY = 4
+HELD = 4
 
 
 def split_pair(value):
@@ -475,10 +476,10 @@
     first, head_count, blocks, owner_ref, weight_ref, mixed_ref, strength_ref, before_ref, *refs
 ):
     *piece_refs, own_ref, other_ref, gram_ref, rows_ref = refs
+    del before_ref
     head = here()
     member = lax.axis_index("member")
     pair_rows, head_size, _ = gram_ref.shape
-    gram_ref[...] = before_ref[...]
     add_pieces(first, owner_ref, weight_ref, piece_refs, gram_ref)
 
     def columns_of(block):
@@ -660,7 +661,7 @@
         return lax.ppermute(pieces[step], ("member", "shard"), pairs)
 
     moved = [pieces[0]] + [move(step) for step in range(1, 1 + EARLY)]
-    tokens, pieces = lax.optimization_barrier((tokens, pieces))
+    tokens, pieces, moved[1] = lax.optimization_barrier((tokens, pieces, moved[1]))
     pack, misc = pl.pallas_call(
         pack_kernel,
         out_shape=(
@@ -723,7 +724,7 @@
         name="project",
     )(packs, misc, *pinned(qkv_weight))
 
-    held = 1 + EARLY
+    held = HELD
     gram = pl.pallas_call(
         gram_kernel,
         out_shape=shape((pair_rows, head_size, 2 * head_size), f32),
@@ -736,18 +737,27 @@
     all_mixed = exchange(mixed, PAIR)
     all_mixed, owner, weight, gram = lax.optimization_barrier((all_mixed, owner, weight, gram))
 
-    own_head, other_head = pl.pallas_call(
+    own_head, other_head, _ = pl.pallas_call(
         functools.partial(solve_kernel, held, head_count, columns // head_size),
-        out_shape=(shape((group_rows, head_size), bf16),) * 2,
+        out_shape=(
+            shape((group_rows, head_size), bf16),
+            shape((group_rows, head_size), bf16),
+            pltpu.VMEM(gram.shape, f32),
+        ),
         in_specs=[SMEM] + [VMEM] * (4 + devices - held),
-        out_specs=(VMEM,) * 2,
-        scratch_shapes=[
-            pltpu.VMEM((pair_rows, head_size, 2 * head_size), f32),
-            pltpu.VMEM((pair_rows, head_size), f32),
-        ],
+        out_specs=(VMEM,) * 3,
+        input_output_aliases={4: 2},
+        scratch_shapes=[pltpu.VMEM((pair_rows, head_size), f32)],
         compiler_params=PARAMS,
         name="solve",
-    )(owner, weight, all_mixed, strength, gram, *moved[held:])
+    )(
+        owner,
+        weight,
+        all_mixed,
+        strength,
+        pltpu.with_memory_space_constraint(gram, pltpu.VMEM),
+        *moved[held:],
+    )
     part = pl.pallas_call(
         out_kernel,
         out_shape=shape((group_rows, width + 2 * head_size), bf16),

time: 54.7 us -> 52.1 us (0.952)
  waiting for transfers between devices: 15.8 us -> 9.34 us
  blocking collectives: 7.25 us -> 10.3 us
  starting transfers between devices: 17.2 us -> 17.9 us
    ppermute x7, waiting for transfers between devices: 7.04 us -> 0.9 us  [move(): return lax.ppermute(pieces[step], ('member', 'shard'), pairs)]
    all_to_all x1, blocking collectives: 7.25 us -> 10.3 us  [exchange(): return lax.all_to_all(value, axes, split_axis=0, concat_axis=0, tiled=True)]
    ppermute x1, starting transfers between devices: 0.67 us -> 1.37 us  [head_body(): lax.ppermute(other_head, 'member', [(0, 1), (1, 0)])]
    ppermute x1, waiting for transfers between devices: 2.98 us -> 2.28 us  [head_body(): lax.ppermute(other_head, 'member', [(0, 1), (1, 0)])]
  transfers between devices with their start and end apart: 15 -> 15, of which waited for: 8 -> 7; matrix products, arithmetic and copies ran while one was open for 0% -> 0% of each run, Pallas kernels for 9% -> 10%
where the time goes in v1:
time: 52.1 us; the launch traced here: 51.7 us
  starting transfers between devices  17.9 us (34%)
  Pallas kernels  13.4 us (26%)
  blocking collectives  10.3 us (20%)
  waiting for transfers between devices  9.34 us (18%)
  between operations  0.74 us (1%)
    all_to_all x1, blocking collectives, exchange(): return lax.all_to_all(value, axes, split_axis=0, concat_axis=0, tiled=True)  10.3 us
    ppermute x7, starting transfers between devices, move(): return lax.ppermute(pieces[step], ('member', 'shard'), pairs)  9.41 us
    ppermute x6, waiting for transfers between devices, over_shards(): arrived.append(lax.ppermute(sent[apart], 'shard', pairs))  4.53 us
    pallas_call x1, Pallas kernels, head_body(): pl.pallas_call(functools.partial(solve_kernel, held, head_count, columns...  4.36 us
    ppermute x6, starting transfers between devices, over_shards(): arrived.append(lax.ppermute(sent[apart], 'shard', pairs))  3.74 us
    all_to_all x1, starting transfers between devices, exchange(): return lax.all_to_all(value, axes, split_axis=0, concat_axis=0, tiled=True)  3.36 us
    ppermute x1, waiting for transfers between devices, head_body(): lax.ppermute(other_head, 'member', [(0, 1), (1, 0)])  2.28 us
    pallas_call x1, Pallas kernels, head_body(): pl.pallas_call(functools.partial(project_kernel, shards, req_rows, slots,...  1.92 us
  transfers between devices with their start and end apart: 15, of which 7 were waited for; matrix products, arithmetic and copies ran while one was open for 0% of the time, Pallas kernels for 10%

profile of v1, /device:TPU:0, one launch (start us, length us, event | category | flops | bytes accessed | tf_op | source)
XLA Modules:
  0.0 51.7 jit_solution(3471614610698524293)
XLA Ops:
  0.6 1.6 %cut.1 = (bf16[8,128,128]{2,1,0:T(8,128)(2,1)S(1)}, bf16[8,128,128]{2,1,0:T(8,128)(2,1)S(1)}, bf16[8,128,128]{2,1,0:T(8,128)(2,1)S(1)}, bf16[8,128,128]{2,1,0:T(...) custom-call(bf16[4,128,1024]{2,1,0:T(8,128)(2,1)} %key_hbm.1, ...), custom_call_target="tpu_custom_call" | custom-call | tf_op jit(solution)/shard_map/cut/pallas_call | solution.py:644
  2.8 3.5 %collective-permute-start.1 = (bf16[8,128,128]{2,1,0:T(8,128)(2,1)S(1)}, bf16[8,128,128]{2,1,0:T(8,128)(2,1)S(1)}, u32[]{:S(2)}, u32[]{:S(2)}) collective-permute-start(bf16[8,128,128]{2,1,0:T(8,128)(2,1)S(1)} %get-tuple-element.42), channel_id=1, source_target_pairs={{0,6},{4,2},{1,7},{5,3},{2,4},{6,0},{3,5},{7,1},{8,14},{12,10},{9,... | collective-permute-start | bytes 786440 | tf_op jit(solution)/shard_map/ppermute | solution.py:661
  6.3 1.6 %pack.1 = (bf16[192,128]{1,0:T(8,128)(2,1)}, f32[32,1024]{1,0:T(8,128)S(1)}) custom-call(bf16[2,1024]{1,0:T(2,128)(2,1)} %tokens_hbm, bf16[4,8,128]{2,1,0:T(8,128)(2,1)} %logs_hbm.1, s32[4]{0:T(128)} %owner_hbm.1, s32[4]{0:T(128)} %fill_hbm.1, bf16[3,8,768]{2,1,0:T(8,128)(2,1)} %bitcast.17, f32[4,768]{1,0:T(4,128)} %tap_hbm.1, f32[1,1024]{1,0:T(1,128)} %bitcast.19, ...), custom_call_target="tpu_custom_call" | custom-call | tf_op jit(solution)/shard_map/pack/pallas_call | solution.py:665
  7.9 3.4 %all-to-all-start = ((bf16[8,24,128]{2,1,0:T(8,128)(2,1)}), bf16[8,24,128]{2,1,0:T(8,128)(2,1)S(1)}, u32[]{:S(2)}, u32[]{:S(2)}) async-start(bf16[8,24,128]{2,1,0:T(8,128)(2,1)} %bitcast.4), calls=%async_computation | async-start | bytes 98304 | tf_op jit(solution)/shard_map/all_to_all | solution.py:632
  11.3 2.6 %collective-permute-start.2 = (bf16[8,128,128]{2,1,0:T(8,128)(2,1)S(1)}, bf16[8,128,128]{2,1,0:T(8,128)(2,1)S(1)}, u32[]{:S(2)}, u32[]{:S(2)}) collective-permute-start(bf16[8,128,128]{2,1,0:T(8,128)(2,1)S(1)} %get-tuple-element.43), channel_id=1, source_target_pairs={{0,7},{4,3},{1,6},{5,2},{2,5},{6,1},{3,4},{7,0},{8,15},{12,11},{9,... | collective-permute-start | bytes 786440 | tf_op jit(solution)/shard_map/ppermute | solution.py:661
  14.4 1.6 %all-to-all-done = bf16[8,24,128]{2,1,0:T(8,128)(2,1)S(1)} async-done(((bf16[8,24,128]{2,1,0:T(8,128)(2,1)}), bf16[8,24,128]{2,1,0:T(8,128)(2,1)S(1)}, u32[]{:S(2)}, u32[]{:S(2)}) %all-to-all-start) | async-done | bytes 49184 | tf_op jit(solution)/shard_map/all_to_all | solution.py:632
  16.5 1.1 %collective-permute-start.5 = (bf16[8,128,128]{2,1,0:T(8,128)(2,1)S(1)}, bf16[8,128,128]{2,1,0:T(8,128)(2,1)S(1)}, u32[]{:S(2)}, u32[]{:S(2)}) collective-permute-start(bf16[8,128,128]{2,1,0:T(8,128)(2,1)S(1)} %get-tuple-element.68), channel_id=1, source_target_pairs={{0,5},{4,1},{1,2},{5,6},{2,7},{6,3},{3,0},{7,4},{8,13},{12,9},{9,1... | collective-permute-start | bytes 786440 | tf_op jit(solution)/shard_map/ppermute | solution.py:661
  17.7 0.6 %collective-permute-start.6 = (bf16[8,128,128]{2,1,0:T(8,128)(2,1)S(1)}, bf16[8,128,128]{2,1,0:T(8,128)(2,1)S(1)}, u32[]{:S(2)}, u32[]{:S(2)}) collective-permute-start(bf16[8,128,128]{2,1,0:T(8,128)(2,1)S(1)} %get-tuple-element.69), channel_id=1, source_target_pairs={{0,3},{4,7},{1,4},{5,0},{2,1},{6,5},{3,6},{7,2},{8,11},{12,15},{9,... | collective-permute-start | bytes 786440 | tf_op jit(solution)/shard_map/ppermute | solution.py:661
  18.3 1.9 %project.1 = (bf16[64,128]{1,0:T(8,128)(2,1)S(1)}, f32[8,1024]{1,0:T(8,128)S(1)}, f32[32,128]{1,0:T(8,128)S(1)}, s32[32,128]{1,0:T(8,128)S(1)}, f32[24,128]{1,0:T(8,128)S(1)}) custom-call(bf16[192,128]{1,0:T(8,128)(2,1)S(1)} %bitcast.13, f32[32,1024]{1,0:T(8,128)S(1)} %get-tuple-element.54.misc_ref, bf16[1024,768]{1,0:T(8,128)(2,1)} %qkv_hbm.1), custom_call_target="tpu_custom_call" | custom-call | tf_op jit(solution)/shard_map/project/pallas_call | solution.py:707
  20.2 0.9 %collective-permute-done.2.refs_3_ = bf16[8,128,128]{2,1,0:T(8,128)(2,1)S(1)} collective-permute-done((bf16[8,128,128]{2,1,0:T(8,128)(2,1)S(1)}, bf16[8,128,128]{2,1,0:T(8,128)(2,1)S(1)}, u32[]{:S(2)}, u32[]{:S(2)}) %collective-permute-start.2) | collective-permute-done | bytes 262176 | tf_op jit(solution)/shard_map/ppermute | solution.py:661
  21.1 1.5 %gram.1.before_ref = f32[16,128,256]{2,1,0:T(8,128)S(1)} custom-call(s32[32,128]{1,0:T(8,128)S(1)} %get-tuple-element.62.owner_ref, f32[32,128]{1,0:T(8,128)S(1)} %get-tuple-element.63.weight_ref, bf16[8,128,128]{2,1,0:T(8,128)(2,1)S(1)} %get-tuple-element.40.refs_0_, bf16[8,128,128]{2,1,0:T(8,128)(2,1)S(1)} %collective-permute-done.refs_1_, ...), custom_call_target="tpu_custom_call" | custom-call | tf_op jit(solution)/shard_map/gram/pallas_call | solution.py:728
  22.6 10.3 %all_to_all.24 = bf16[8,8,128]{2,1,0:T(8,128)(2,1)S(1)} all-to-all(bf16[8,8,128]{2,1,0:T(8,128)(2,1)S(1)} %bitcast.15), channel_id=1, replica_groups=mesh['pair'=4,'member'=2,'shard'=4] {'shard','member'}, dimensions={0} | all-to-all | bytes 32768 | tf_op jit(solution)/shard_map/all_to_all | solution.py:632
  32.9 4.4 %solve.1 = (bf16[8,128]{1,0:T(8,128)(2,1)S(1)}, bf16[8,128]{1,0:T(8,128)(2,1)S(1)}, f32[16,128,256]{2,1,0:T(8,128)S(1)}) custom-call(s32[32,128]{1,0:T(8,128)S(1)} %get-tuple-element.62.owner_ref, f32[32,128]{1,0:T(8,128)S(1)} %get-tuple-element.63.weight_ref, bf16[64,128]{1,0:T(8,128)(2,1)S(1)} %bitcast.14, ...), custom_call_target="tpu_custom_call", output_to_operand_aliasing={{2}: (4, {})} | custom-call | tf_op jit(solution)/shard_map/solve/pallas_call | solution.py:740
  37.3 1.4 %collective-permute-start.7 = (bf16[8,128]{1,0:T(8,128)(2,1)S(1)}, bf16[8,128]{1,0:T(8,128)(2,1)S(1)}, u32[]{:S(2)}, u32[]{:S(2)}) collective-permute-start(bf16[8,128]{1,0:T(8,128)(2,1)S(1)} %get-tuple-element.71), channel_id=1, source_target_pairs={{0,4},{4,0},{1,5},{5,1},{2,6},{6,2},{3,7},{7,3},{8,12},{12,8},{9,1... | collective-permute-start | bytes 6152 | tf_op jit(solution)/shard_map/ppermute | solution.py:768
  38.7 2.3 %collective-permute-done.7.come_ref = bf16[8,128]{1,0:T(8,128)(2,1)S(1)} collective-permute-done((bf16[8,128]{1,0:T(8,128)(2,1)S(1)}, bf16[8,128]{1,0:T(8,128)(2,1)S(1)}, u32[]{:S(2)}, u32[]{:S(2)}) %collective-permute-start.7) | collective-permute-done | bytes 2080 | tf_op jit(solution)/shard_map/ppermute | solution.py:768
  41.1 1.3 %collective-permute-start.9 = (bf16[8,1280]{1,0:T(8,128)(2,1)S(1)}, bf16[8,1280]{1,0:T(8,128)(2,1)S(1)}, u32[]{:S(2)}, u32[]{:S(2)}) collective-permute-start(bf16[8,1280]{1,0:T(8,128)(2,1)S(1)} %out.1.refs_0_), channel_id=1, source_target_pairs={{0,2},{1,3},{2,0},{3,1},{4,6},{5,7},{6,4},{7,5},{8,10},{9,11},{10,... | collective-permute-start | bytes 61448 | tf_op jit(solution)/shard_map/ppermute | solution.py:774
  42.4 0.6 %collective-permute-start.8 = (bf16[8,1280]{1,0:T(8,128)(2,1)S(1)}, bf16[8,1280]{1,0:T(8,128)(2,1)S(1)}, u32[]{:S(2)}, u32[]{:S(2)}) collective-permute-start(bf16[8,1280]{1,0:T(8,128)(2,1)S(1)} %out.1.refs_0_), channel_id=1, source_target_pairs={{0,1},{1,0},{2,3},{3,2},{4,5},{5,4},{6,7},{7,6},{8,9},{9,8},{10,11... | collective-permute-start | bytes 61448 | tf_op jit(solution)/shard_map/ppermute | solution.py:774
  43.0 1.4 %collective-permute-done.10.refs_3_ = bf16[8,1280]{1,0:T(8,128)(2,1)S(1)} collective-permute-done((bf16[8,1280]{1,0:T(8,128)(2,1)S(1)}, bf16[8,1280]{1,0:T(8,128)(2,1)S(1)}, u32[]{:S(2)}, u32[]{:S(2)}) %collective-permute-start.10) | collective-permute-done | bytes 20512 | tf_op jit(solution)/shard_map/ppermute | solution.py:774
  44.4 0.6 %collective-permute-done.9.refs_2_ = bf16[8,1280]{1,0:T(8,128)(2,1)S(1)} collective-permute-done((bf16[8,1280]{1,0:T(8,128)(2,1)S(1)}, bf16[8,1280]{1,0:T(8,128)(2,1)S(1)}, u32[]{:S(2)}, u32[]{:S(2)}) %collective-permute-start.9) | collective-permute-done | bytes 20512 | tf_op jit(solution)/shard_map/ppermute | solution.py:774
  45.0 1.7 %mlp.1 = (f32[2,1024]{1,0:T(2,128)S(1)}, bf16[2,1024]{1,0:T(2,128)(2,1)}, f32[16,128]{1,0:T(8,128)S(1)}, f32[16,128]{1,0:T(8,128)S(1)}, f32[16,128]{1,0:T(8,128)S(1)}, /*index=5*/f32[16,128]{1,0:T(8,128)S(1)}) custom-call(f32[8,1024]{1,0:T(8,128)S(1)} %get-tuple-element.55.tokens_ref, f32[1,1024]{1,0:T(1,128)S(1)} %bitcast.16, ...), custom_call_target="tpu_custom_call" | custom-call | tf_op jit(solution)/shard_map/mlp/pallas_call | solution.py:779
  46.8 1.2 %collective-permute-start.12 = (f32[16,128]{1,0:T(8,128)S(1)}, f32[16,128]{1,0:T(8,128)S(1)}, u32[]{:S(2)}, u32[]{:S(2)}) collective-permute-start(f32[16,128]{1,0:T(8,128)S(1)} %get-tuple-element.76), channel_id=1, source_target_pairs={{0,2},{1,3},{2,0},{3,1},{4,6},{5,7},{6,4},{7,5},{8,10},{9,11},{10,... | collective-permute-start | bytes 24584 | tf_op jit(solution)/shard_map/ppermute | solution.py:774
  48.5 2.0 %collective-permute-done.12.refs_2_ = f32[16,128]{1,0:T(8,128)S(1)} collective-permute-done((f32[16,128]{1,0:T(8,128)S(1)}, f32[16,128]{1,0:T(8,128)S(1)}, u32[]{:S(2)}, u32[]{:S(2)}) %collective-permute-start.12) | collective-permute-done | bytes 8224 | tf_op jit(solution)/shard_map/ppermute | solution.py:774
  50.5 0.6 %collective-permute-done.13.refs_3_ = f32[16,128]{1,0:T(8,128)S(1)} collective-permute-done((f32[16,128]{1,0:T(8,128)S(1)}, f32[16,128]{1,0:T(8,128)S(1)}, u32[]{:S(2)}, u32[]{:S(2)}) %collective-permute-start.13) | collective-permute-done | bytes 8224 | tf_op jit(solution)/shard_map/ppermute | solution.py:774
  51.1 0.6 %finish.1 = bf16[2,1024]{1,0:T(2,128)(2,1)} custom-call(f32[2,1024]{1,0:T(2,128)S(1)} %get-tuple-element.73.mid_ref, f32[16,128]{1,0:T(8,128)S(1)} %get-tuple-element.74.refs_0_, f32[16,128]{1,0:T(8,128)S(1)} %collective-permute-done.11.refs_1_, f32[16,128]{1,0:T(8,128)S(1)} %collective-permute-done.12.refs_2_, f32[16,128]{1,0:T(8,128)S(1)} %collective-permute-done.13.refs_3_), custom_call_target="tpu_custom_call" | custom-call | tf_op jit(solution)/shard_map/finish/pallas_call | solution.py:802
  (25 shorter events, 2.4 us)
Async XLA Ops:
  2.3 4.0 %collective-permute-start = (bf16[8,128,128]{2,1,0:T(8,128)(2,1)S(1)}, bf16[8,128,128]{2,1,0:T(8,128)(2,1)S(1)}, u32[]{:S(2)}, u32[]{:S(2)}) collective-permute-start(bf16[8,128,128]{2,1,0:T(8,128)(2,1)S(1)} %get-tuple-element.41), channel_id=1, source_target_pairs={{0,1},{4,5},{1,0},{5,4},{2,3},{6,7},{3,2},{7,6},{8,9},{12,13},{9,8... | collective-permute-start | bytes 786440 | tf_op jit(solution)/shard_map/ppermute | solution.py:661
  2.8 14.9 %collective-permute-start.1 = (bf16[8,128,128]{2,1,0:T(8,128)(2,1)S(1)}, bf16[8,128,128]{2,1,0:T(8,128)(2,1)S(1)}, u32[]{:S(2)}, u32[]{:S(2)}) collective-permute-start(bf16[8,128,128]{2,1,0:T(8,128)(2,1)S(1)} %get-tuple-element.42), channel_id=1, source_target_pairs={{0,6},{4,2},{1,7},{5,3},{2,4},{6,0},{3,5},{7,1},{8,14},{12,10},{9,... | collective-permute-start | bytes 786440 | tf_op jit(solution)/shard_map/ppermute | solution.py:661
  7.9 8.1 %all-to-all-start = ((bf16[8,24,128]{2,1,0:T(8,128)(2,1)}), bf16[8,24,128]{2,1,0:T(8,128)(2,1)S(1)}, u32[]{:S(2)}, u32[]{:S(2)}) async-start(bf16[8,24,128]{2,1,0:T(8,128)(2,1)} %bitcast.4), calls=%async_computation | async-start | bytes 98304 | tf_op jit(solution)/shard_map/all_to_all | solution.py:632
  11.3 9.8 %collective-permute-start.2 = (bf16[8,128,128]{2,1,0:T(8,128)(2,1)S(1)}, bf16[8,128,128]{2,1,0:T(8,128)(2,1)S(1)}, u32[]{:S(2)}, u32[]{:S(2)}) collective-permute-start(bf16[8,128,128]{2,1,0:T(8,128)(2,1)S(1)} %get-tuple-element.43), channel_id=1, source_target_pairs={{0,7},{4,3},{1,6},{5,2},{2,5},{6,1},{3,4},{7,0},{8,15},{12,11},{9,... | collective-permute-start | bytes 786440 | tf_op jit(solution)/shard_map/ppermute | solution.py:661
  13.9 19.0 %collective-permute-start.3 = (bf16[8,128,128]{2,1,0:T(8,128)(2,1)S(1)}, bf16[8,128,128]{2,1,0:T(8,128)(2,1)S(1)}, u32[]{:S(2)}, u32[]{:S(2)}) collective-permute-start(bf16[8,128,128]{2,1,0:T(8,128)(2,1)S(1)} %get-tuple-element.44), channel_id=1, source_target_pairs={{0,4},{4,0},{1,3},{5,7},{2,6},{6,2},{3,1},{7,5},{8,12},{12,8},{9,1... | collective-permute-start | bytes 786440 | tf_op jit(solution)/shard_map/ppermute | solution.py:661
  16.1 16.8 %collective-permute-start.4 = (bf16[8,128,128]{2,1,0:T(8,128)(2,1)S(1)}, bf16[8,128,128]{2,1,0:T(8,128)(2,1)S(1)}, u32[]{:S(2)}, u32[]{:S(2)}) collective-permute-start(bf16[8,128,128]{2,1,0:T(8,128)(2,1)S(1)} %get-tuple-element.67), channel_id=1, source_target_pairs={{0,2},{4,6},{1,5},{5,1},{2,0},{6,4},{3,7},{7,3},{8,10},{12,14},{9,... | collective-permute-start | bytes 786440 | tf_op jit(solution)/shard_map/ppermute | solution.py:661
  16.5 16.4 %collective-permute-start.5 = (bf16[8,128,128]{2,1,0:T(8,128)(2,1)S(1)}, bf16[8,128,128]{2,1,0:T(8,128)(2,1)S(1)}, u32[]{:S(2)}, u32[]{:S(2)}) collective-permute-start(bf16[8,128,128]{2,1,0:T(8,128)(2,1)S(1)} %get-tuple-element.68), channel_id=1, source_target_pairs={{0,5},{4,1},{1,2},{5,6},{2,7},{6,3},{3,0},{7,4},{8,13},{12,9},{9,1... | collective-permute-start | bytes 786440 | tf_op jit(solution)/shard_map/ppermute | solution.py:661
  17.7 15.2 %collective-permute-start.6 = (bf16[8,128,128]{2,1,0:T(8,128)(2,1)S(1)}, bf16[8,128,128]{2,1,0:T(8,128)(2,1)S(1)}, u32[]{:S(2)}, u32[]{:S(2)}) collective-permute-start(bf16[8,128,128]{2,1,0:T(8,128)(2,1)S(1)} %get-tuple-element.69), channel_id=1, source_target_pairs={{0,3},{4,7},{1,4},{5,0},{2,1},{6,5},{3,6},{7,2},{8,11},{12,15},{9,... | collective-permute-start | bytes 786440 | tf_op jit(solution)/shard_map/ppermute | solution.py:661
  21.1 19.9 %copy-start.3 = (bf16[256,1024]{1,0:T(8,128)(2,1)S(1)}, bf16[256,1024]{1,0:T(8,128)(2,1)}, u32[]{:S(2)}) copy-start(bf16[256,1024]{1,0:T(8,128)(2,1)} %out_ref.1) | copy-start | bytes 1572868
  21.1 23.9 %copy-start.2 = (bf16[704,1024]{1,0:T(8,128)(2,1)S(1)}, bf16[704,1024]{1,0:T(8,128)(2,1)}, u32[]{:S(2)}) copy-start(bf16[704,1024]{1,0:T(8,128)(2,1)} %down_ref.1) | copy-start | bytes 4325380
  32.9 12.1 %copy-start = (bf16[1024,704]{0,1:T(8,128)(2,1)S(1)}, bf16[1024,704]{0,1:T(8,128)(2,1)}, u32[]{:S(2)}) copy-start(bf16[1024,704]{0,1:T(8,128)(2,1)} %param.33) | copy-start | bytes 4325380
  32.9 12.1 %copy-start.1 = (bf16[1024,704]{0,1:T(8,128)(2,1)S(1)}, bf16[1024,704]{0,1:T(8,128)(2,1)}, u32[]{:S(2)}) copy-start(bf16[1024,704]{0,1:T(8,128)(2,1)} %param.34) | copy-start | bytes 4325380
  32.9 12.1 %copy-start.4 = (f32[1024]{0:T(1024)S(1)}, f32[1024]{0:T(1024)}, u32[]{:S(2)}) copy-start(f32[1024]{0:T(1024)} %param.32) | copy-start | bytes 12292
  37.3 3.7 %collective-permute-start.7 = (bf16[8,128]{1,0:T(8,128)(2,1)S(1)}, bf16[8,128]{1,0:T(8,128)(2,1)S(1)}, u32[]{:S(2)}, u32[]{:S(2)}) collective-permute-start(bf16[8,128]{1,0:T(8,128)(2,1)S(1)} %get-tuple-element.71), channel_id=1, source_target_pairs={{0,4},{4,0},{1,5},{5,1},{2,6},{6,2},{3,7},{7,3},{8,12},{12,8},{9,1... | collective-permute-start | bytes 6152 | tf_op jit(solution)/shard_map/ppermute | solution.py:768
  41.1 3.2 %collective-permute-start.10 = (bf16[8,1280]{1,0:T(8,128)(2,1)S(1)}, bf16[8,1280]{1,0:T(8,128)(2,1)S(1)}, u32[]{:S(2)}, u32[]{:S(2)}) collective-permute-start(bf16[8,1280]{1,0:T(8,128)(2,1)S(1)} %out.1.refs_0_), channel_id=1, source_target_pairs={{0,3},{1,2},{2,1},{3,0},{4,7},{5,6},{6,5},{7,4},{8,11},{9,10},{10,... | collective-permute-start | bytes 61448 | tf_op jit(solution)/shard_map/ppermute | solution.py:774
  41.1 3.8 %collective-permute-start.9 = (bf16[8,1280]{1,0:T(8,128)(2,1)S(1)}, bf16[8,1280]{1,0:T(8,128)(2,1)S(1)}, u32[]{:S(2)}, u32[]{:S(2)}) collective-permute-start(bf16[8,1280]{1,0:T(8,128)(2,1)S(1)} %out.1.refs_0_), channel_id=1, source_target_pairs={{0,2},{1,3},{2,0},{3,1},{4,6},{5,7},{6,4},{7,5},{8,10},{9,11},{10,... | collective-permute-start | bytes 61448 | tf_op jit(solution)/shard_map/ppermute | solution.py:774
  42.4 2.5 %collective-permute-start.8 = (bf16[8,1280]{1,0:T(8,128)(2,1)S(1)}, bf16[8,1280]{1,0:T(8,128)(2,1)S(1)}, u32[]{:S(2)}, u32[]{:S(2)}) collective-permute-start(bf16[8,1280]{1,0:T(8,128)(2,1)S(1)} %out.1.refs_0_), channel_id=1, source_target_pairs={{0,1},{1,0},{2,3},{3,2},{4,5},{5,4},{6,7},{7,6},{8,9},{9,8},{10,11... | collective-permute-start | bytes 61448 | tf_op jit(solution)/shard_map/ppermute | solution.py:774
  46.7 1.9 %collective-permute-start.11 = (f32[16,128]{1,0:T(8,128)S(1)}, f32[16,128]{1,0:T(8,128)S(1)}, u32[]{:S(2)}, u32[]{:S(2)}) collective-permute-start(f32[16,128]{1,0:T(8,128)S(1)} %get-tuple-element.75), channel_id=1, source_target_pairs={{0,1},{1,0},{2,3},{3,2},{4,5},{5,4},{6,7},{7,6},{8,9},{9,8},{10,11... | collective-permute-start | bytes 24584 | tf_op jit(solution)/shard_map/ppermute | solution.py:774
  46.8 3.7 %collective-permute-start.12 = (f32[16,128]{1,0:T(8,128)S(1)}, f32[16,128]{1,0:T(8,128)S(1)}, u32[]{:S(2)}, u32[]{:S(2)}) collective-permute-start(f32[16,128]{1,0:T(8,128)S(1)} %get-tuple-element.76), channel_id=1, source_target_pairs={{0,2},{1,3},{2,0},{3,1},{4,6},{5,7},{6,4},{7,5},{8,10},{9,11},{10,... | collective-permute-start | bytes 24584 | tf_op jit(solution)/shard_map/ppermute | solution.py:774
  48.0 3.1 %collective-permute-start.13 = (f32[16,128]{1,0:T(8,128)S(1)}, f32[16,128]{1,0:T(8,128)S(1)}, u32[]{:S(2)}, u32[]{:S(2)}) collective-permute-start(f32[16,128]{1,0:T(8,128)S(1)} %get-tuple-element.77), channel_id=1, source_target_pairs={{0,3},{1,2},{2,1},{3,0},{4,7},{5,6},{6,5},{7,4},{8,11},{9,10},{10,... | collective-permute-start | bytes 24584 | tf_op jit(solution)/shard_map/ppermute | solution.py:774

commit v2 on v1

--- a/solution.py
+++ b/solution.py
@@ -196,7 +196,7 @@
 PAST, TAP, GAIN, BIAS, RIDGE = slice(0, 8), slice(8, 9), slice(9, 10), slice(10, 11), slice(11, 12)
 GATES = slice(16, 32)
 
-SEND = ((0, 0), (2, 2), (5, 5), (7, 7), (1, 4), (4, 1), (3, 6), (6, 3))
+SEND = ((0, 0), (5, 5), (2, 2), (7, 7), (1, 4), (4, 1), (3, 6), (6, 3))
 FROM = tuple((b, a) if a & 2 else (a, b) for a, b in SEND)
 EARLY = 4
 HELD = 4
@@ -661,7 +661,7 @@
         return lax.ppermute(pieces[step], ("member", "shard"), pairs)
 
     moved = [pieces[0]] + [move(step) for step in range(1, 1 + EARLY)]
-    tokens, pieces, moved[1] = lax.optimization_barrier((tokens, pieces, moved[1]))
+    tokens, pieces = lax.optimization_barrier((tokens, pieces))
     pack, misc = pl.pallas_call(
         pack_kernel,
         out_shape=(

time: 52.1 us -> 52 us (level)
  no operation moved by 1% of the time
where the time goes in v2:
time: 52 us; the launch traced here: 51.6 us
  starting transfers between devices  17.8 us (34%)
  Pallas kernels  13.4 us (26%)
  blocking collectives  10.3 us (20%)
  waiting for transfers between devices  9.33 us (18%)
  between operations  0.74 us (1%)
    all_to_all x1, blocking collectives, exchange(): return lax.all_to_all(value, axes, split_axis=0, concat_axis=0, tiled=True)  10.3 us
    ppermute x7, starting transfers between devices, move(): return lax.ppermute(pieces[step], ('member', 'shard'), pairs)  9.34 us
    ppermute x6, waiting for transfers between devices, over_shards(): arrived.append(lax.ppermute(sent[apart], 'shard', pairs))  4.53 us
    pallas_call x1, Pallas kernels, head_body(): pl.pallas_call(functools.partial(solve_kernel, held, head_count, columns...  4.36 us
    ppermute x6, starting transfers between devices, over_shards(): arrived.append(lax.ppermute(sent[apart], 'shard', pairs))  3.74 us
    all_to_all x1, starting transfers between devices, exchange(): return lax.all_to_all(value, axes, split_axis=0, concat_axis=0, tiled=True)  3.36 us
    ppermute x1, waiting for transfers between devices, head_body(): lax.ppermute(other_head, 'member', [(0, 1), (1, 0)])  2.28 us
    pallas_call x1, Pallas kernels, head_body(): pl.pallas_call(functools.partial(project_kernel, shards, req_rows, slots,...  1.92 us
  transfers between devices with their start and end apart: 15, of which 7 were waited for; matrix products, arithmetic and copies ran while one was open for 0% of the time, Pallas kernels for 10%

profile of v2, /device:TPU:0, one launch (start us, length us, event | category | flops | bytes accessed | tf_op | source)
XLA Modules:
  0.0 51.6 jit_solution(12344862175475364160)
XLA Ops:
  0.6 1.6 %cut.1 = (bf16[8,128,128]{2,1,0:T(8,128)(2,1)S(1)}, bf16[8,128,128]{2,1,0:T(8,128)(2,1)S(1)}, bf16[8,128,128]{2,1,0:T(8,128)(2,1)S(1)}, bf16[8,128,128]{2,1,0:T(...) custom-call(bf16[4,128,1024]{2,1,0:T(8,128)(2,1)} %key_hbm.1, ...), custom_call_target="tpu_custom_call" | custom-call | tf_op jit(solution)/shard_map/cut/pallas_call | solution.py:644
  2.3 4.0 %collective-permute-start = (bf16[8,128,128]{2,1,0:T(8,128)(2,1)S(1)}, bf16[8,128,128]{2,1,0:T(8,128)(2,1)S(1)}, u32[]{:S(2)}, u32[]{:S(2)}) collective-permute-start(bf16[8,128,128]{2,1,0:T(8,128)(2,1)S(1)} %get-tuple-element.40), channel_id=1, source_target_pairs={{0,6},{4,2},{1,7},{5,3},{2,4},{6,0},{3,5},{7,1},{8,14},{12,10},{9,... | collective-permute-start | bytes 786440 | tf_op jit(solution)/shard_map/ppermute | solution.py:661
  6.2 1.6 %pack.1 = (bf16[192,128]{1,0:T(8,128)(2,1)}, f32[32,1024]{1,0:T(8,128)S(1)}) custom-call(bf16[2,1024]{1,0:T(2,128)(2,1)} %tokens_hbm, bf16[4,8,128]{2,1,0:T(8,128)(2,1)} %logs_hbm.1, s32[4]{0:T(128)} %owner_hbm.1, s32[4]{0:T(128)} %fill_hbm.1, bf16[3,8,768]{2,1,0:T(8,128)(2,1)} %bitcast.17, f32[4,768]{1,0:T(4,128)} %tap_hbm.1, f32[1,1024]{1,0:T(1,128)} %bitcast.19, ...), custom_call_target="tpu_custom_call" | custom-call | tf_op jit(solution)/shard_map/pack/pallas_call | solution.py:665
  7.8 3.4 %all-to-all-start = ((bf16[8,24,128]{2,1,0:T(8,128)(2,1)}), bf16[8,24,128]{2,1,0:T(8,128)(2,1)S(1)}, u32[]{:S(2)}, u32[]{:S(2)}) async-start(bf16[8,24,128]{2,1,0:T(8,128)(2,1)} %bitcast.4), calls=%async_computation | async-start | bytes 98304 | tf_op jit(solution)/shard_map/all_to_all | solution.py:632
  11.2 2.6 %collective-permute-start.2 = (bf16[8,128,128]{2,1,0:T(8,128)(2,1)S(1)}, bf16[8,128,128]{2,1,0:T(8,128)(2,1)S(1)}, u32[]{:S(2)}, u32[]{:S(2)}) collective-permute-start(bf16[8,128,128]{2,1,0:T(8,128)(2,1)S(1)} %get-tuple-element.42), channel_id=1, source_target_pairs={{0,7},{4,3},{1,6},{5,2},{2,5},{6,1},{3,4},{7,0},{8,15},{12,11},{9,... | collective-permute-start | bytes 786440 | tf_op jit(solution)/shard_map/ppermute | solution.py:661
  14.4 1.6 %all-to-all-done = bf16[8,24,128]{2,1,0:T(8,128)(2,1)S(1)} async-done(((bf16[8,24,128]{2,1,0:T(8,128)(2,1)}), bf16[8,24,128]{2,1,0:T(8,128)(2,1)S(1)}, u32[]{:S(2)}, u32[]{:S(2)}) %all-to-all-start) | async-done | bytes 49184 | tf_op jit(solution)/shard_map/all_to_all | solution.py:632
  16.5 1.1 %collective-permute-start.5 = (bf16[8,128,128]{2,1,0:T(8,128)(2,1)S(1)}, bf16[8,128,128]{2,1,0:T(8,128)(2,1)S(1)}, u32[]{:S(2)}, u32[]{:S(2)}) collective-permute-start(bf16[8,128,128]{2,1,0:T(8,128)(2,1)S(1)} %get-tuple-element.66), channel_id=1, source_target_pairs={{0,5},{4,1},{1,2},{5,6},{2,7},{6,3},{3,0},{7,4},{8,13},{12,9},{9,1... | collective-permute-start | bytes 786440 | tf_op jit(solution)/shard_map/ppermute | solution.py:661
  17.6 0.6 %collective-permute-start.6 = (bf16[8,128,128]{2,1,0:T(8,128)(2,1)S(1)}, bf16[8,128,128]{2,1,0:T(8,128)(2,1)S(1)}, u32[]{:S(2)}, u32[]{:S(2)}) collective-permute-start(bf16[8,128,128]{2,1,0:T(8,128)(2,1)S(1)} %get-tuple-element.67), channel_id=1, source_target_pairs={{0,3},{4,7},{1,4},{5,0},{2,1},{6,5},{3,6},{7,2},{8,11},{12,15},{9,... | collective-permute-start | bytes 786440 | tf_op jit(solution)/shard_map/ppermute | solution.py:661
  18.2 1.9 %project.1 = (bf16[64,128]{1,0:T(8,128)(2,1)S(1)}, f32[8,1024]{1,0:T(8,128)S(1)}, f32[32,128]{1,0:T(8,128)S(1)}, s32[32,128]{1,0:T(8,128)S(1)}, f32[24,128]{1,0:T(8,128)S(1)}) custom-call(bf16[192,128]{1,0:T(8,128)(2,1)S(1)} %bitcast.13, f32[32,1024]{1,0:T(8,128)S(1)} %get-tuple-element.53.misc_ref, bf16[1024,768]{1,0:T(8,128)(2,1)} %qkv_hbm.1), custom_call_target="tpu_custom_call" | custom-call | tf_op jit(solution)/shard_map/project/pallas_call | solution.py:707
  20.1 0.9 %collective-permute-done.2.refs_3_ = bf16[8,128,128]{2,1,0:T(8,128)(2,1)S(1)} collective-permute-done((bf16[8,128,128]{2,1,0:T(8,128)(2,1)S(1)}, bf16[8,128,128]{2,1,0:T(8,128)(2,1)S(1)}, u32[]{:S(2)}, u32[]{:S(2)}) %collective-permute-start.2) | collective-permute-done | bytes 262176 | tf_op jit(solution)/shard_map/ppermute | solution.py:661
  21.0 1.5 %gram.1.before_ref = f32[16,128,256]{2,1,0:T(8,128)S(1)} custom-call(s32[32,128]{1,0:T(8,128)S(1)} %get-tuple-element.60.owner_ref, f32[32,128]{1,0:T(8,128)S(1)} %get-tuple-element.61.weight_ref, bf16[8,128,128]{2,1,0:T(8,128)(2,1)S(1)} %get-tuple-element.39.refs_0_, bf16[8,128,128]{2,1,0:T(8,128)(2,1)S(1)} %collective-permute-done.refs_1_, ...), custom_call_target="tpu_custom_call" | custom-call | tf_op jit(solution)/shard_map/gram/pallas_call | solution.py:728
  22.5 10.3 %all_to_all.24 = bf16[8,8,128]{2,1,0:T(8,128)(2,1)S(1)} all-to-all(bf16[8,8,128]{2,1,0:T(8,128)(2,1)S(1)} %bitcast.15), channel_id=1, replica_groups=mesh['pair'=4,'member'=2,'shard'=4] {'shard','member'}, dimensions={0} | all-to-all | bytes 32768 | tf_op jit(solution)/shard_map/all_to_all | solution.py:632
  32.9 4.4 %solve.1 = (bf16[8,128]{1,0:T(8,128)(2,1)S(1)}, bf16[8,128]{1,0:T(8,128)(2,1)S(1)}, f32[16,128,256]{2,1,0:T(8,128)S(1)}) custom-call(s32[32,128]{1,0:T(8,128)S(1)} %get-tuple-element.60.owner_ref, f32[32,128]{1,0:T(8,128)S(1)} %get-tuple-element.61.weight_ref, bf16[64,128]{1,0:T(8,128)(2,1)S(1)} %bitcast.14, ...), custom_call_target="tpu_custom_call", output_to_operand_aliasing={{2}: (4, {})} | custom-call | tf_op jit(solution)/shard_map/solve/pallas_call | solution.py:740
  37.2 1.4 %collective-permute-start.7 = (bf16[8,128]{1,0:T(8,128)(2,1)S(1)}, bf16[8,128]{1,0:T(8,128)(2,1)S(1)}, u32[]{:S(2)}, u32[]{:S(2)}) collective-permute-start(bf16[8,128]{1,0:T(8,128)(2,1)S(1)} %get-tuple-element.69), channel_id=1, source_target_pairs={{0,4},{4,0},{1,5},{5,1},{2,6},{6,2},{3,7},{7,3},{8,12},{12,8},{9,1... | collective-permute-start | bytes 6152 | tf_op jit(solution)/shard_map/ppermute | solution.py:768
  38.6 2.3 %collective-permute-done.7.come_ref = bf16[8,128]{1,0:T(8,128)(2,1)S(1)} collective-permute-done((bf16[8,128]{1,0:T(8,128)(2,1)S(1)}, bf16[8,128]{1,0:T(8,128)(2,1)S(1)}, u32[]{:S(2)}, u32[]{:S(2)}) %collective-permute-start.7) | collective-permute-done | bytes 2080 | tf_op jit(solution)/shard_map/ppermute | solution.py:768
  41.0 1.3 %collective-permute-start.9 = (bf16[8,1280]{1,0:T(8,128)(2,1)S(1)}, bf16[8,1280]{1,0:T(8,128)(2,1)S(1)}, u32[]{:S(2)}, u32[]{:S(2)}) collective-permute-start(bf16[8,1280]{1,0:T(8,128)(2,1)S(1)} %out.1.refs_0_), channel_id=1, source_target_pairs={{0,2},{1,3},{2,0},{3,1},{4,6},{5,7},{6,4},{7,5},{8,10},{9,11},{10,... | collective-permute-start | bytes 61448 | tf_op jit(solution)/shard_map/ppermute | solution.py:774
  42.4 0.6 %collective-permute-start.8 = (bf16[8,1280]{1,0:T(8,128)(2,1)S(1)}, bf16[8,1280]{1,0:T(8,128)(2,1)S(1)}, u32[]{:S(2)}, u32[]{:S(2)}) collective-permute-start(bf16[8,1280]{1,0:T(8,128)(2,1)S(1)} %out.1.refs_0_), channel_id=1, source_target_pairs={{0,1},{1,0},{2,3},{3,2},{4,5},{5,4},{6,7},{7,6},{8,9},{9,8},{10,11... | collective-permute-start | bytes 61448 | tf_op jit(solution)/shard_map/ppermute | solution.py:774
  42.9 1.4 %collective-permute-done.10.refs_3_ = bf16[8,1280]{1,0:T(8,128)(2,1)S(1)} collective-permute-done((bf16[8,1280]{1,0:T(8,128)(2,1)S(1)}, bf16[8,1280]{1,0:T(8,128)(2,1)S(1)}, u32[]{:S(2)}, u32[]{:S(2)}) %collective-permute-start.10) | collective-permute-done | bytes 20512 | tf_op jit(solution)/shard_map/ppermute | solution.py:774
  44.3 0.6 %collective-permute-done.9.refs_2_ = bf16[8,1280]{1,0:T(8,128)(2,1)S(1)} collective-permute-done((bf16[8,1280]{1,0:T(8,128)(2,1)S(1)}, bf16[8,1280]{1,0:T(8,128)(2,1)S(1)}, u32[]{:S(2)}, u32[]{:S(2)}) %collective-permute-start.9) | collective-permute-done | bytes 20512 | tf_op jit(solution)/shard_map/ppermute | solution.py:774
  44.9 1.7 %mlp.1 = (f32[2,1024]{1,0:T(2,128)S(1)}, bf16[2,1024]{1,0:T(2,128)(2,1)}, f32[16,128]{1,0:T(8,128)S(1)}, f32[16,128]{1,0:T(8,128)S(1)}, f32[16,128]{1,0:T(8,128)S(1)}, /*index=5*/f32[16,128]{1,0:T(8,128)S(1)}) custom-call(f32[8,1024]{1,0:T(8,128)S(1)} %get-tuple-element.54.tokens_ref, f32[1,1024]{1,0:T(1,128)S(1)} %bitcast.16, ...), custom_call_target="tpu_custom_call" | custom-call | tf_op jit(solution)/shard_map/mlp/pallas_call | solution.py:779
  46.8 1.2 %collective-permute-start.12 = (f32[16,128]{1,0:T(8,128)S(1)}, f32[16,128]{1,0:T(8,128)S(1)}, u32[]{:S(2)}, u32[]{:S(2)}) collective-permute-start(f32[16,128]{1,0:T(8,128)S(1)} %get-tuple-element.74), channel_id=1, source_target_pairs={{0,2},{1,3},{2,0},{3,1},{4,6},{5,7},{6,4},{7,5},{8,10},{9,11},{10,... | collective-permute-start | bytes 24584 | tf_op jit(solution)/shard_map/ppermute | solution.py:774
  48.5 2.0 %collective-permute-done.12.refs_2_ = f32[16,128]{1,0:T(8,128)S(1)} collective-permute-done((f32[16,128]{1,0:T(8,128)S(1)}, f32[16,128]{1,0:T(8,128)S(1)}, u32[]{:S(2)}, u32[]{:S(2)}) %collective-permute-start.12) | collective-permute-done | bytes 8224 | tf_op jit(solution)/shard_map/ppermute | solution.py:774
  50.4 0.6 %collective-permute-done.13.refs_3_ = f32[16,128]{1,0:T(8,128)S(1)} collective-permute-done((f32[16,128]{1,0:T(8,128)S(1)}, f32[16,128]{1,0:T(8,128)S(1)}, u32[]{:S(2)}, u32[]{:S(2)}) %collective-permute-start.13) | collective-permute-done | bytes 8224 | tf_op jit(solution)/shard_map/ppermute | solution.py:774
  51.0 0.6 %finish.1 = bf16[2,1024]{1,0:T(2,128)(2,1)} custom-call(f32[2,1024]{1,0:T(2,128)S(1)} %get-tuple-element.71.mid_ref, f32[16,128]{1,0:T(8,128)S(1)} %get-tuple-element.72.refs_0_, f32[16,128]{1,0:T(8,128)S(1)} %collective-permute-done.11.refs_1_, f32[16,128]{1,0:T(8,128)S(1)} %collective-permute-done.12.refs_2_, f32[16,128]{1,0:T(8,128)S(1)} %collective-permute-done.13.refs_3_), custom_call_target="tpu_custom_call" | custom-call | tf_op jit(solution)/shard_map/finish/pallas_call | solution.py:802
  (25 shorter events, 1.9 us)
Async XLA Ops:
  2.3 14.2 %collective-permute-start = (bf16[8,128,128]{2,1,0:T(8,128)(2,1)S(1)}, bf16[8,128,128]{2,1,0:T(8,128)(2,1)S(1)}, u32[]{:S(2)}, u32[]{:S(2)}) collective-permute-start(bf16[8,128,128]{2,1,0:T(8,128)(2,1)S(1)} %get-tuple-element.40), channel_id=1, source_target_pairs={{0,6},{4,2},{1,7},{5,3},{2,4},{6,0},{3,5},{7,1},{8,14},{12,10},{9,... | collective-permute-start | bytes 786440 | tf_op jit(solution)/shard_map/ppermute | solution.py:661
  6.2 11.3 %collective-permute-start.1 = (bf16[8,128,128]{2,1,0:T(8,128)(2,1)S(1)}, bf16[8,128,128]{2,1,0:T(8,128)(2,1)S(1)}, u32[]{:S(2)}, u32[]{:S(2)}) collective-permute-start(bf16[8,128,128]{2,1,0:T(8,128)(2,1)S(1)} %get-tuple-element.41), channel_id=1, source_target_pairs={{0,1},{4,5},{1,0},{5,4},{2,3},{6,7},{3,2},{7,6},{8,9},{12,13},{9,8... | collective-permute-start | bytes 786440 | tf_op jit(solution)/shard_map/ppermute | solution.py:661
  7.8 8.1 %all-to-all-start = ((bf16[8,24,128]{2,1,0:T(8,128)(2,1)}), bf16[8,24,128]{2,1,0:T(8,128)(2,1)S(1)}, u32[]{:S(2)}, u32[]{:S(2)}) async-start(bf16[8,24,128]{2,1,0:T(8,128)(2,1)} %bitcast.4), calls=%async_computation | async-start | bytes 98304 | tf_op jit(solution)/shard_map/all_to_all | solution.py:632
  11.2 9.8 %collective-permute-start.2 = (bf16[8,128,128]{2,1,0:T(8,128)(2,1)S(1)}, bf16[8,128,128]{2,1,0:T(8,128)(2,1)S(1)}, u32[]{:S(2)}, u32[]{:S(2)}) collective-permute-start(bf16[8,128,128]{2,1,0:T(8,128)(2,1)S(1)} %get-tuple-element.42), channel_id=1, source_target_pairs={{0,7},{4,3},{1,6},{5,2},{2,5},{6,1},{3,4},{7,0},{8,15},{12,11},{9,... | collective-permute-start | bytes 786440 | tf_op jit(solution)/shard_map/ppermute | solution.py:661
  13.8 19.0 %collective-permute-start.3 = (bf16[8,128,128]{2,1,0:T(8,128)(2,1)S(1)}, bf16[8,128,128]{2,1,0:T(8,128)(2,1)S(1)}, u32[]{:S(2)}, u32[]{:S(2)}) collective-permute-start(bf16[8,128,128]{2,1,0:T(8,128)(2,1)S(1)} %get-tuple-element.43), channel_id=1, source_target_pairs={{0,4},{4,0},{1,3},{5,7},{2,6},{6,2},{3,1},{7,5},{8,12},{12,8},{9,1... | collective-permute-start | bytes 786440 | tf_op jit(solution)/shard_map/ppermute | solution.py:661
  16.0 16.8 %collective-permute-start.4 = (bf16[8,128,128]{2,1,0:T(8,128)(2,1)S(1)}, bf16[8,128,128]{2,1,0:T(8,128)(2,1)S(1)}, u32[]{:S(2)}, u32[]{:S(2)}) collective-permute-start(bf16[8,128,128]{2,1,0:T(8,128)(2,1)S(1)} %get-tuple-element.65), channel_id=1, source_target_pairs={{0,2},{4,6},{1,5},{5,1},{2,0},{6,4},{3,7},{7,3},{8,10},{12,14},{9,... | collective-permute-start | bytes 786440 | tf_op jit(solution)/shard_map/ppermute | solution.py:661
  16.5 16.4 %collective-permute-start.5 = (bf16[8,128,128]{2,1,0:T(8,128)(2,1)S(1)}, bf16[8,128,128]{2,1,0:T(8,128)(2,1)S(1)}, u32[]{:S(2)}, u32[]{:S(2)}) collective-permute-start(bf16[8,128,128]{2,1,0:T(8,128)(2,1)S(1)} %get-tuple-element.66), channel_id=1, source_target_pairs={{0,5},{4,1},{1,2},{5,6},{2,7},{6,3},{3,0},{7,4},{8,13},{12,9},{9,1... | collective-permute-start | bytes 786440 | tf_op jit(solution)/shard_map/ppermute | solution.py:661
  17.6 15.2 %collective-permute-start.6 = (bf16[8,128,128]{2,1,0:T(8,128)(2,1)S(1)}, bf16[8,128,128]{2,1,0:T(8,128)(2,1)S(1)}, u32[]{:S(2)}, u32[]{:S(2)}) collective-permute-start(bf16[8,128,128]{2,1,0:T(8,128)(2,1)S(1)} %get-tuple-element.67), channel_id=1, source_target_pairs={{0,3},{4,7},{1,4},{5,0},{2,1},{6,5},{3,6},{7,2},{8,11},{12,15},{9,... | collective-permute-start | bytes 786440 | tf_op jit(solution)/shard_map/ppermute | solution.py:661
  21.0 19.9 %copy-start.3 = (bf16[256,1024]{1,0:T(8,128)(2,1)S(1)}, bf16[256,1024]{1,0:T(8,128)(2,1)}, u32[]{:S(2)}) copy-start(bf16[256,1024]{1,0:T(8,128)(2,1)} %out_ref.1) | copy-start | bytes 1572868
  21.0 23.9 %copy-start.2 = (bf16[704,1024]{1,0:T(8,128)(2,1)S(1)}, bf16[704,1024]{1,0:T(8,128)(2,1)}, u32[]{:S(2)}) copy-start(bf16[704,1024]{1,0:T(8,128)(2,1)} %down_ref.1) | copy-start | bytes 4325380
  32.8 12.1 %copy-start = (bf16[1024,704]{0,1:T(8,128)(2,1)S(1)}, bf16[1024,704]{0,1:T(8,128)(2,1)}, u32[]{:S(2)}) copy-start(bf16[1024,704]{0,1:T(8,128)(2,1)} %param.33) | copy-start | bytes 4325380
  32.8 12.1 %copy-start.1 = (bf16[1024,704]{0,1:T(8,128)(2,1)S(1)}, bf16[1024,704]{0,1:T(8,128)(2,1)}, u32[]{:S(2)}) copy-start(bf16[1024,704]{0,1:T(8,128)(2,1)} %param.34) | copy-start | bytes 4325380
  32.8 12.1 %copy-start.4 = (f32[1024]{0:T(1024)S(1)}, f32[1024]{0:T(1024)}, u32[]{:S(2)}) copy-start(f32[1024]{0:T(1024)} %param.32) | copy-start | bytes 12292
  37.2 3.7 %collective-permute-start.7 = (bf16[8,128]{1,0:T(8,128)(2,1)S(1)}, bf16[8,128]{1,0:T(8,128)(2,1)S(1)}, u32[]{:S(2)}, u32[]{:S(2)}) collective-permute-start(bf16[8,128]{1,0:T(8,128)(2,1)S(1)} %get-tuple-element.69), channel_id=1, source_target_pairs={{0,4},{4,0},{1,5},{5,1},{2,6},{6,2},{3,7},{7,3},{8,12},{12,8},{9,1... | collective-permute-start | bytes 6152 | tf_op jit(solution)/shard_map/ppermute | solution.py:768
  41.0 3.2 %collective-permute-start.10 = (bf16[8,1280]{1,0:T(8,128)(2,1)S(1)}, bf16[8,1280]{1,0:T(8,128)(2,1)S(1)}, u32[]{:S(2)}, u32[]{:S(2)}) collective-permute-start(bf16[8,1280]{1,0:T(8,128)(2,1)S(1)} %out.1.refs_0_), channel_id=1, source_target_pairs={{0,3},{1,2},{2,1},{3,0},{4,7},{5,6},{6,5},{7,4},{8,11},{9,10},{10,... | collective-permute-start | bytes 61448 | tf_op jit(solution)/shard_map/ppermute | solution.py:774
  41.0 3.8 %collective-permute-start.9 = (bf16[8,1280]{1,0:T(8,128)(2,1)S(1)}, bf16[8,1280]{1,0:T(8,128)(2,1)S(1)}, u32[]{:S(2)}, u32[]{:S(2)}) collective-permute-start(bf16[8,1280]{1,0:T(8,128)(2,1)S(1)} %out.1.refs_0_), channel_id=1, source_target_pairs={{0,2},{1,3},{2,0},{3,1},{4,6},{5,7},{6,4},{7,5},{8,10},{9,11},{10,... | collective-permute-start | bytes 61448 | tf_op jit(solution)/shard_map/ppermute | solution.py:774
  42.4 2.5 %collective-permute-start.8 = (bf16[8,1280]{1,0:T(8,128)(2,1)S(1)}, bf16[8,1280]{1,0:T(8,128)(2,1)S(1)}, u32[]{:S(2)}, u32[]{:S(2)}) collective-permute-start(bf16[8,1280]{1,0:T(8,128)(2,1)S(1)} %out.1.refs_0_), channel_id=1, source_target_pairs={{0,1},{1,0},{2,3},{3,2},{4,5},{5,4},{6,7},{7,6},{8,9},{9,8},{10,11... | collective-permute-start | bytes 61448 | tf_op jit(solution)/shard_map/ppermute | solution.py:774
  46.6 1.9 %collective-permute-start.11 = (f32[16,128]{1,0:T(8,128)S(1)}, f32[16,128]{1,0:T(8,128)S(1)}, u32[]{:S(2)}, u32[]{:S(2)}) collective-permute-start(f32[16,128]{1,0:T(8,128)S(1)} %get-tuple-element.73), channel_id=1, source_target_pairs={{0,1},{1,0},{2,3},{3,2},{4,5},{5,4},{6,7},{7,6},{8,9},{9,8},{10,11... | collective-permute-start | bytes 24584 | tf_op jit(solution)/shard_map/ppermute | solution.py:774
  46.8 3.7 %collective-permute-start.12 = (f32[16,128]{1,0:T(8,128)S(1)}, f32[16,128]{1,0:T(8,128)S(1)}, u32[]{:S(2)}, u32[]{:S(2)}) collective-permute-start(f32[16,128]{1,0:T(8,128)S(1)} %get-tuple-element.74), channel_id=1, source_target_pairs={{0,2},{1,3},{2,0},{3,1},{4,6},{5,7},{6,4},{7,5},{8,10},{9,11},{10,... | collective-permute-start | bytes 24584 | tf_op jit(solution)/shard_map/ppermute | solution.py:774
  47.9 3.1 %collective-permute-start.13 = (f32[16,128]{1,0:T(8,128)S(1)}, f32[16,128]{1,0:T(8,128)S(1)}, u32[]{:S(2)}, u32[]{:S(2)}) collective-permute-start(f32[16,128]{1,0:T(8,128)S(1)} %get-tuple-element.75), channel_id=1, source_target_pairs={{0,3},{1,2},{2,1},{3,0},{4,7},{5,6},{6,5},{7,4},{8,11},{9,10},{10,... | collective-permute-start | bytes 24584 | tf_op jit(solution)/shard_map/ppermute | solution.py:774
